TPU v7x, 32 devices: a whole 2x2x4 slice. The times are simulated.
32 devices in a mesh: dp: 4 (over y, x), seq: 8 (over z, core).
Axes of the slice: x: 2, y: 2, z: 4, core: 2. Of those that a mesh axis runs over, the one named last changes fastest.
Arguments:
- tokens: bfloat16 [4, 1024, 1024], P('dp', 'seq'), may hold values from -7 to 7
- cotangent: bfloat16 [4, 1024, 1024], P('dp', 'seq'), may hold values from -6 to 6
- weight_qkv: float32 [1024, 3072], P(('dp', 'seq')), may hold values from -0.1875 to 0.1875
- weight_out: float32 [1024, 1024], P(('dp', 'seq')), may hold values from -3.5 to 3.5
- weight_up: float32 [1024, 4096], P(('dp', 'seq')), may hold values from -0.1875 to 0.1875
- weight_down: float32 [4096, 1024], P(('dp', 'seq')), may hold values from -0.09375 to 0.09375
- small_params: float32 [1024, 12], P(('dp', 'seq')), may hold values from -1.3 to 3, as said below
- moment_qkv: float32 [1024, 3072], P(('dp', 'seq')), may hold values from -0.0017089844 to 0.0017089844
- moment_out: float32 [1024, 1024], P(('dp', 'seq')), may hold values from -9.1552734e-05 to 9.1552734e-05
- moment_up: float32 [1024, 4096], P(('dp', 'seq')), may hold values from -0.0017089844 to 0.0017089844
- moment_down: float32 [4096, 1024], P(('dp', 'seq')), may hold values from -0.0017089844 to 0.0017089844
- moment_small: float32 [1024, 12], P(('dp', 'seq')), may hold values from -0.0034179688 to 0.0034179688
- second_qkv: float32 [1024, 3072], P(('dp', 'seq')), may hold values from 6.510417e-08 to 2.6200456e-07
- second_out: float32 [1024, 1024], P(('dp', 'seq')), may hold values from 1.9036306e-10 to 7.6609524e-10
- second_up: float32 [1024, 4096], P(('dp', 'seq')), may hold values from 6.510417e-08 to 2.6200456e-07
- second_down: float32 [4096, 1024], P(('dp', 'seq')), may hold values from 6.510417e-08 to 2.6200456e-07
- second_small: float32 [1024, 12], P(('dp', 'seq')), may hold values from 2.6200456e-07 to 1.0321393e-06
Outputs:
- layer_output: bfloat16 [4, 1024, 1024], P('dp', 'seq')
- grad_tokens: float32 [4, 1024, 1024], P('dp', 'seq')
- grad_norm: float32 [], replicated
- new_qkv: float32 [1024, 3072], P(('dp', 'seq'))
- new_out: float32 [1024, 1024], P(('dp', 'seq'))
- new_up: float32 [1024, 4096], P(('dp', 'seq'))
- new_down: float32 [4096, 1024], P(('dp', 'seq'))
- new_small: float32 [1024, 12], P(('dp', 'seq'))
- new_moment_qkv: float32 [1024, 3072], P(('dp', 'seq'))
- new_moment_out: float32 [1024, 1024], P(('dp', 'seq'))
- new_moment_up: float32 [1024, 4096], P(('dp', 'seq'))
- new_moment_down: float32 [4096, 1024], P(('dp', 'seq'))
- new_moment_small: float32 [1024, 12], P(('dp', 'seq'))
- new_second_qkv: float32 [1024, 3072], P(('dp', 'seq'))
- new_second_out: float32 [1024, 1024], P(('dp', 'seq'))
- new_second_up: float32 [1024, 4096], P(('dp', 'seq'))
- new_second_down: float32 [4096, 1024], P(('dp', 'seq'))
- new_second_small: float32 [1024, 12], P(('dp', 'seq'))
Inputs may be any that keep to these rules, and one draw needn't show every extreme that they name: `small_params`: gain columns are positive.
All inputs are finite; a program needn't handle non-finite values.
Results may differ from a plain program's by a relative error of at most 0.015.
Values may be sent and summed in bfloat16 or wider, within the bound.
No kernel may reach another device: no remote copies, remote signals or barrier semaphores. Data moves between devices by JAX's collectives and lax.ppermute only.
A program may use at most 192 MiB of HBM per device.

v0:
```python
import jax
import jax.numpy as jnp
from jax import lax
from jax.sharding import PartitionSpec as P

HEAD = 64
STEP = 5


NORM_EPSILON = 1e-05
ADAM_EPSILON = 1e-08
BETA_FIRST = 0.5
BETA_SECOND = 0.55
CLIP_LIMIT = 1.0
RATE_MATRIX = 0.04
RATE_OUTPUT = 0.5
RATE_SMALL = 0.3
WEIGHT_DECAY = 0.01
SCORE_SCALE = 0.125


def layer_norm(value, gain, shift):
    center = jnp.mean(value, axis=-1, keepdims=True)
    centered = value - center
    variance = jnp.mean(centered * centered, axis=-1, keepdims=True)
    return centered * lax.rsqrt(variance + NORM_EPSILON) * gain + shift


def exact_gelu(value):
    return jax.nn.gelu(value, approximate=False)


def unpack(table_low):
    table = table_low.astype(jnp.float32)
    ratio = table.shape[1] - 8
    bias_up = table[:, 3 : 3 + ratio].T.reshape(-1)
    return (
        table[:, 0],
        table[:, 1],
        table[:, 2],
        bias_up,
        table[:, 3 + ratio],
        table[:, 4 + ratio],
        table[:, 5 + ratio],
        table[:, 6 + ratio],
        table[:, 7 + ratio],
    )


def cross(left, right):
    return lax.dot_general(
        left, right, (((0,), (0,)), ((), ())), preferred_element_type=jnp.float32
    )


def against(left, right):
    return lax.dot_general(
        left, right, (((1,), (1,)), ((), ())), preferred_element_type=jnp.float32
    )


def take_block(source, index, block, heads):
    piece = lax.dynamic_slice_in_dim(source, index * block, block, 0)
    return piece.reshape(block, heads, HEAD)


def scores_of(query_heads, key_heads):
    return (
        jnp.einsum("qhd,khd->hqk", query_heads, key_heads, preferred_element_type=jnp.float32)
        * SCORE_SCALE
    )


def block_grads(query_heads, key_heads, value_heads, dout_heads, log_total, delta):
    scores = scores_of(query_heads, key_heads)
    probs = jnp.exp(scores - log_total[..., None])
    grad_probs = jnp.einsum(
        "qhd,khd->hqk", dout_heads, value_heads, preferred_element_type=jnp.float32
    )
    grad_scores = (probs * (grad_probs - delta[..., None])).astype(jnp.bfloat16)
    return (probs, grad_scores)


def attention_forward(query_heads, keys_all, values_all, block):
    count_rows, heads = (query_heads.shape[0], query_heads.shape[1])
    count = keys_all.shape[0] // block

    def stats_step(index, carry):
        run_top, run_total = carry
        scores = scores_of(query_heads, take_block(keys_all, index, block, heads))
        new_top = jnp.maximum(run_top, jnp.max(scores, axis=-1))
        run_total = run_total * jnp.exp(run_top - new_top) + jnp.sum(
            jnp.exp(scores - new_top[..., None]), axis=-1
        )
        return (new_top, run_total)

    start_top = jnp.full((heads, count_rows), -1e30, jnp.float32)
    start_total = jnp.zeros((heads, count_rows), jnp.float32)
    run_top, run_total = lax.fori_loop(0, count, stats_step, (start_top, start_total))
    log_total = run_top + jnp.log(run_total)

    def value_step(index, accum):
        scores = scores_of(query_heads, take_block(keys_all, index, block, heads))
        weights = jnp.exp(scores - log_total[..., None]).astype(jnp.bfloat16)
        return accum + jnp.einsum(
            "hqk,khd->qhd",
            weights,
            take_block(values_all, index, block, heads),
            preferred_element_type=jnp.float32,
        )

    accum = lax.fori_loop(0, count, value_step, jnp.zeros((count_rows, heads, HEAD), jnp.float32))
    return (accum.reshape(count_rows, heads * HEAD), log_total)


def adam_update(weight, grad, moment, second, rate, decay):
    moment_new = BETA_FIRST * moment + (1.0 - BETA_FIRST) * grad
    second_new = BETA_SECOND * second + (1.0 - BETA_SECOND) * grad * grad
    direction = (
        moment_new
        / (1.0 - BETA_FIRST**STEP)
        / (jnp.sqrt(second_new / (1.0 - BETA_SECOND**STEP)) + ADAM_EPSILON)
    )
    return (weight - rate * (direction + decay * weight), moment_new, second_new)


def on_device(
    tokens,
    cotangent,
    weight_qkv,
    weight_out,
    weight_up,
    weight_down,
    small_params,
    moment_qkv,
    moment_out,
    moment_up,
    moment_down,
    moment_small,
    second_qkv,
    second_out,
    second_up,
    second_down,
    second_small,
):
    rows = tokens[0]
    count_rows = rows.shape[0]
    width = rows.shape[1]
    heads = width // HEAD
    block = 4 * count_rows
    full_qkv, full_out, full_up, full_down, full_small = (
        lax.all_gather(weight_qkv.astype(jnp.bfloat16), ("dp", "seq"), axis=0, tiled=True),
        lax.all_gather(weight_out.astype(jnp.bfloat16), ("dp", "seq"), axis=0, tiled=True),
        lax.all_gather(weight_up.astype(jnp.bfloat16), ("dp", "seq"), axis=0, tiled=True),
        lax.all_gather(weight_down.astype(jnp.bfloat16), ("dp", "seq"), axis=0, tiled=True),
        lax.all_gather(small_params.astype(jnp.bfloat16), ("dp", "seq"), axis=0, tiled=True),
    )
    (
        bias_query,
        bias_value,
        bias_out,
        bias_up,
        bias_down,
        gain_one,
        shift_one,
        gain_two,
        shift_two,
    ) = unpack(full_small)
    projected = jnp.dot(rows, full_qkv, preferred_element_type=jnp.float32)
    query = (projected[:, :width] + bias_query).astype(jnp.bfloat16)
    key_rows = projected[:, width : 2 * width].astype(jnp.bfloat16)
    value_rows = (projected[:, 2 * width :] + bias_value).astype(jnp.bfloat16)
    keys_all, values_all = (
        lax.all_gather(key_rows, "seq", axis=0, tiled=True),
        lax.all_gather(value_rows, "seq", axis=0, tiled=True),
    )
    query_heads = query.reshape(count_rows, heads, HEAD)
    attended, log_total = attention_forward(query_heads, keys_all, values_all, block)
    attended_low = attended.astype(jnp.bfloat16)
    branch = jnp.dot(attended_low, full_out, preferred_element_type=jnp.float32) + bias_out
    middle = rows.astype(jnp.float32) + branch
    hidden, norm_one_back = jax.vjp(layer_norm, middle, gain_one, shift_one)
    hidden_low = hidden.astype(jnp.bfloat16)
    upward = jnp.dot(hidden_low, full_up, preferred_element_type=jnp.float32) + bias_up
    activation, gelu_back = jax.vjp(exact_gelu, upward)
    activation_low = activation.astype(jnp.bfloat16)
    downward = jnp.dot(activation_low, full_down, preferred_element_type=jnp.float32) + bias_down
    output, norm_two_back = jax.vjp(layer_norm, hidden + downward, gain_two, shift_two)
    back_qkv, back_out, back_up, back_down = (
        lax.all_gather(weight_qkv.astype(jnp.bfloat16), ("dp", "seq"), axis=0, tiled=True),
        lax.all_gather(weight_out.astype(jnp.bfloat16), ("dp", "seq"), axis=0, tiled=True),
        lax.all_gather(weight_up.astype(jnp.bfloat16), ("dp", "seq"), axis=0, tiled=True),
        lax.all_gather(weight_down.astype(jnp.bfloat16), ("dp", "seq"), axis=0, tiled=True),
    )
    grad_sum_two, grad_gain_two, grad_shift_two = norm_two_back(cotangent[0].astype(jnp.float32))
    grad_down_low = grad_sum_two.astype(jnp.bfloat16)
    grad_bias_down = jnp.sum(grad_down_low.astype(jnp.float32), axis=0)
    grad_weight_down = cross(activation_low, grad_down_low)
    grad_activation = against(grad_down_low, back_down)
    grad_up_low = gelu_back(grad_activation)[0].astype(jnp.bfloat16)
    grad_bias_up = jnp.sum(grad_up_low.astype(jnp.float32), axis=0)
    grad_weight_up = cross(hidden_low, grad_up_low)
    grad_hidden = grad_sum_two + against(grad_up_low, back_up)
    grad_middle, grad_gain_one, grad_shift_one = norm_one_back(grad_hidden)
    grad_branch_low = grad_middle.astype(jnp.bfloat16)
    grad_bias_out = jnp.sum(grad_branch_low.astype(jnp.float32), axis=0)
    grad_weight_out = cross(attended_low, grad_branch_low)
    grad_attended = against(grad_branch_low, back_out).astype(jnp.bfloat16)
    delta = jnp.sum(
        (grad_attended.astype(jnp.float32) * attended).reshape(count_rows, heads, HEAD), axis=-1
    ).T
    dout_heads = grad_attended.reshape(count_rows, heads, HEAD)
    count = keys_all.shape[0] // block

    def both_step(index, carry):
        grad_query, grad_keys, grad_values = carry
        key_heads = take_block(keys_all, index, block, heads)
        value_heads = take_block(values_all, index, block, heads)
        probs, grad_scores = block_grads(
            query_heads, key_heads, value_heads, dout_heads, log_total, delta
        )
        grad_query = (
            grad_query
            + jnp.einsum("hqk,khd->qhd", grad_scores, key_heads, preferred_element_type=jnp.float32)
            * SCORE_SCALE
        )
        part_keys = (
            jnp.einsum("hqk,qhd->khd", grad_scores, query_heads, preferred_element_type=jnp.float32)
            * SCORE_SCALE
        )
        part_values = jnp.einsum(
            "hqk,qhd->khd",
            probs.astype(jnp.bfloat16),
            dout_heads,
            preferred_element_type=jnp.float32,
        )
        grad_keys = lax.dynamic_update_slice_in_dim(
            grad_keys, part_keys.reshape(block, width), index * block, 0
        )
        grad_values = lax.dynamic_update_slice_in_dim(
            grad_values, part_values.reshape(block, width), index * block, 0
        )
        return (grad_query, grad_keys, grad_values)

    start = (
        jnp.zeros((count_rows, heads, HEAD), jnp.float32),
        jnp.zeros((keys_all.shape[0], width), jnp.float32),
        jnp.zeros((keys_all.shape[0], width), jnp.float32),
    )
    grad_query, grad_keys, grad_values = lax.fori_loop(0, count, both_step, start)
    summed_keys, summed_values = (
        lax.psum_scatter(
            grad_keys.astype(jnp.bfloat16), "seq", scatter_dimension=0, tiled=True
        ).astype(jnp.float32),
        lax.psum_scatter(
            grad_values.astype(jnp.bfloat16), "seq", scatter_dimension=0, tiled=True
        ).astype(jnp.float32),
    )
    grad_query_low = grad_query.reshape(count_rows, width).astype(jnp.bfloat16)
    grad_value_low = summed_values.astype(jnp.bfloat16)
    grad_projected = jnp.concatenate(
        [grad_query_low, summed_keys.astype(jnp.bfloat16), grad_value_low], axis=1
    )
    grad_weight_qkv = cross(rows, grad_projected)
    grad_bias_query = jnp.sum(grad_query_low.astype(jnp.float32), axis=0)
    grad_bias_value = jnp.sum(grad_value_low.astype(jnp.float32), axis=0)
    grad_rows = grad_middle + against(grad_projected, back_qkv)
    ratio = full_up.shape[1] // width
    grad_small = jnp.concatenate(
        [
            jnp.stack([grad_bias_query, grad_bias_value, grad_bias_out], axis=1),
            grad_bias_up.reshape(ratio, width).T,
            jnp.stack(
                [grad_bias_down, grad_gain_one, grad_shift_one, grad_gain_two, grad_shift_two],
                axis=1,
            ),
        ],
        axis=1,
    )
    owned_qkv, owned_out, owned_up, owned_down, owned_small = (
        lax.psum_scatter(grad_weight_qkv, ("dp", "seq"), scatter_dimension=0, tiled=True),
        lax.psum_scatter(grad_weight_out, ("dp", "seq"), scatter_dimension=0, tiled=True),
        lax.psum_scatter(grad_weight_up, ("dp", "seq"), scatter_dimension=0, tiled=True),
        lax.psum_scatter(grad_weight_down, ("dp", "seq"), scatter_dimension=0, tiled=True),
        lax.psum_scatter(grad_small, ("dp", "seq"), scatter_dimension=0, tiled=True),
    )
    squares = jnp.sum(owned_qkv * owned_qkv) + jnp.sum(owned_out * owned_out)
    squares = squares + jnp.sum(owned_up * owned_up) + jnp.sum(owned_down * owned_down)
    squares = squares + jnp.sum(owned_small * owned_small)
    total = lax.psum(squares, ("dp", "seq"))
    grad_norm = jnp.sqrt(total)
    factor = jnp.minimum(1.0, CLIP_LIMIT / (grad_norm + 1e-06))
    new_qkv, new_moment_qkv, new_second_qkv = adam_update(
        weight_qkv, owned_qkv * factor, moment_qkv, second_qkv, RATE_MATRIX, WEIGHT_DECAY
    )
    new_out, new_moment_out, new_second_out = adam_update(
        weight_out, owned_out * factor, moment_out, second_out, RATE_OUTPUT, WEIGHT_DECAY
    )
    new_up, new_moment_up, new_second_up = adam_update(
        weight_up, owned_up * factor, moment_up, second_up, RATE_MATRIX, WEIGHT_DECAY
    )
    new_down, new_moment_down, new_second_down = adam_update(
        weight_down, owned_down * factor, moment_down, second_down, RATE_MATRIX, WEIGHT_DECAY
    )
    new_small, new_moment_small, new_second_small = adam_update(
        small_params, owned_small * factor, moment_small, second_small, RATE_SMALL, 0.0
    )
    return (
        output.astype(jnp.bfloat16)[None],
        grad_rows[None],
        grad_norm,
        new_qkv,
        new_out,
        new_up,
        new_down,
        new_small,
        new_moment_qkv,
        new_moment_out,
        new_moment_up,
        new_moment_down,
        new_moment_small,
        new_second_qkv,
        new_second_out,
        new_second_up,
        new_second_down,
        new_second_small,
    )


def solution(mesh):
    in_specs = (
        P("dp", "seq", None),
        P("dp", "seq", None),
        P(("dp", "seq"), None),
        P(("dp", "seq"), None),
        P(("dp", "seq"), None),
        P(("dp", "seq"), None),
        P(("dp", "seq"), None),
        P(("dp", "seq"), None),
        P(("dp", "seq"), None),
        P(("dp", "seq"), None),
        P(("dp", "seq"), None),
        P(("dp", "seq"), None),
        P(("dp", "seq"), None),
        P(("dp", "seq"), None),
        P(("dp", "seq"), None),
        P(("dp", "seq"), None),
        P(("dp", "seq"), None),
    )
    out_specs = (
        P("dp", "seq", None),
        P("dp", "seq", None),
        P(),
        P(("dp", "seq"), None),
        P(("dp", "seq"), None),
        P(("dp", "seq"), None),
        P(("dp", "seq"), None),
        P(("dp", "seq"), None),
        P(("dp", "seq"), None),
        P(("dp", "seq"), None),
        P(("dp", "seq"), None),
        P(("dp", "seq"), None),
        P(("dp", "seq"), None),
        P(("dp", "seq"), None),
        P(("dp", "seq"), None),
        P(("dp", "seq"), None),
        P(("dp", "seq"), None),
        P(("dp", "seq"), None),
    )
    return jax.shard_map(
        on_device, mesh=mesh, in_specs=in_specs, out_specs=out_specs, check_vma=False
    )
```

profile of v0, /device:TPU:0, one launch (start us, length us, event | category | flops | bytes accessed | tf_op | source)
XLA Modules:
  0.0 1365.1 jit_solution(16030669379247451078)
XLA Ops:
  9.7 44.2 %all-gather = bf16[32,32,12]{1,2,0:T(8,128)(2,1)S(1)} all-gather(bf16[1,32,12]{1,2,0:T(8,128)(2,1)S(1)} %convert_bitcast_fusion.1), channel_id=1, replica_groups=mesh['dp'=4,'seq'=8] {'dp','seq'}, dimensions={0}, use_global_device_ids=true | all-gather | bytes 25344 | tf_op jit(solution)/shard_map/all_gather | solution.py:156
  54.0 30.0 %all-gather.8.cloned.1.call-done = bf16[1024,3072]{1,0:T(8,128)(2,1)} async-done(((bf16[32,3072]{1,0:T(8,128)(2,1)}), bf16[1024,3072]{1,0:T(8,128)(2,1)}) %all-gather.8.cloned.1.call-update) | async-done | bytes 6291472 | tf_op jit(solution)/shard_map/all_gather | solution.py:152
  84.1 3.9 fusion.38
  92.3 24.3 %all-gather.10.cloned.1.call-done = bf16[1024,1024]{1,0:T(8,128)(2,1)} async-done(((bf16[128,1024]{1,0:T(8,128)(2,1)}), bf16[1024,1024]{1,0:T(8,128)(2,1)}) %all-gather.10.cloned.1.call-update) | async-done | bytes 2097168 | tf_op jit(solution)/shard_map/all_gather | solution.py:175
  116.6 3.9 copy.88
  120.5 26.9 %all-gather.12.cloned.1.call-done = bf16[1024,1024]{1,0:T(8,128)(2,1)} async-done(((bf16[128,1024]{1,0:T(8,128)(2,1)}), bf16[1024,1024]{1,0:T(8,128)(2,1)}) %all-gather.12.cloned.1.call-update) | async-done | bytes 2097168 | tf_op jit(solution)/shard_map/all_gather | solution.py:174
  147.4 2.9 copy.89
  150.2 11.7 while.48
  150.4 2.8 bitcast_reduce_fusion.3
  153.1 2.9 fusion.118
  156.2 2.8 bitcast_reduce_fusion.3
  159.0 2.9 fusion.118
  162.0 11.7 while.49
  162.0 2.4 constant_dynamic-slice_fusion.10
  164.4 3.4 fusion.123
  167.8 2.4 constant_dynamic-slice_fusion.10
  170.2 3.5 fusion.123
  174.9 31.8 %all-gather.14.cloned.1.call-done = bf16[1024,1024]{1,0:T(8,128)(2,1)} async-done(((bf16[32,1024]{1,0:T(8,128)(2,1)}), bf16[1024,1024]{1,0:T(8,128)(2,1)}) %all-gather.14.cloned.1.call-update) | async-done | bytes 2097168 | tf_op jit(solution)/shard_map/all_gather | solution.py:153
  206.8 2.3 fusion.61
  209.3 77.0 %all-gather.16.cloned.1.call-done = bf16[1024,4096]{1,0:T(8,128)(2,1)} async-done(((bf16[32,4096]{1,0:T(8,128)(2,1)}), bf16[1024,4096]{1,0:T(8,128)(2,1)}) %all-gather.16.cloned.1.call-update) | async-done | bytes 8388624 | tf_op jit(solution)/shard_map/all_gather | solution.py:154
  286.3 9.8 multiply_convert_fusion.1
  296.1 69.7 %all-gather.18.cloned.1.call-done = bf16[4096,1024]{1,0:T(8,128)(2,1)} async-done(((bf16[128,1024]{1,0:T(8,128)(2,1)}), bf16[4096,1024]{1,0:T(8,128)(2,1)}) %all-gather.18.cloned.1.call-update) | async-done | bytes 8388624 | tf_op jit(solution)/shard_map/all_gather | solution.py:155
  365.8 5.3 fusion.62
  372.7 5.9 convert_reduce_fusion
  378.7 3.1 multiply_reduce_fusion.1
  385.2 1.8 copy.90
  390.5 25.5 %while.50 = (s32[]{:T(128)}, f32[128,16,64]{0,2,1:T(8,128)}, bf16[1024,1024]{0,1:T(8,128)(2,1)}, bf16[1024,1024]{0,1:T(8,128)(2,1)}, bf16[1024,1024]{0,1:T(8,128...) while((s32[]{:T(128)}, f32[128,16,64]{0,2,1:T(8,128)}, ...), condition=%wide.region_16.0_spmd.clone, body=%wide.region_15.0_spmd.clone.sunk | while | flops 680919040 | bytes 127951344 | solution.py:250
  397.3 2.0 fusion.136
  407.4 2.5 fusion.135
  410.0 2.0 fusion.136
  416.0 3.9 copy.98
  421.5 2.6 copy.96
  425.6 28.9 %reduce-scatter.24.cloned.1.call-done = bf16[128,1024]{1,0:T(8,128)(2,1)} async-done(((bf16[1024,1024]{1,0:T(8,128)(2,1)}), bf16[128,1024]{1,0:T(8,128)(2,1)}) %reduce-scatter.24.cloned.1.call-update) | async-done | bytes 262160
  457.0 2.7 fusion.41
  459.7 31.5 %reduce-scatter.22.cloned.1.call-done = bf16[128,1024]{1,0:T(8,128)(2,1)} async-done(((bf16[1024,1024]{1,0:T(8,128)(2,1)}), bf16[128,1024]{1,0:T(8,128)(2,1)}) %reduce-scatter.22.cloned.1.call-update) | async-done | bytes 262160
  492.4 6.3 convolution_bitcast_fusion
  498.7 12.6 copy.100
  512.7 8.2 fusion.49
  522.1 8.1 fusion.64
  530.3 96.4 %reduce-scatter.28.cloned.1.call-done = f32[32,12]{1,0:T(8,128)} async-done(((f32[1024,12]{1,0:T(8,128)}), f32[32,12]{1,0:T(8,128)}) %reduce-scatter.28.cloned.1.call-update) | async-done | bytes 1552
  628.1 139.8 %reduce-scatter.16.cloned.1.call-done = f32[32,1024]{1,0:T(8,128)} async-done(((f32[1024,1024]{1,0:T(8,128)}), f32[32,1024]{1,0:T(8,128)}) %reduce-scatter.16.cloned.1.call-update) | async-done | bytes 131088 | tf_op jit(solution)/shard_map/reduce_scatter | solution.py:282
  769.5 158.2 %reduce-scatter.26.cloned.1.call-done = f32[32,3072]{1,0:T(8,128)} async-done(((f32[1024,3072]{1,0:T(8,128)}), f32[32,3072]{1,0:T(8,128)}) %reduce-scatter.26.cloned.1.call-update) | async-done | bytes 393232 | tf_op jit(solution)/shard_map/reduce_scatter | solution.py:281
  931.4 184.2 %reduce-scatter.18.cloned.1.call-done = f32[32,4096]{1,0:T(8,128)} async-done(((f32[1024,4096]{1,0:T(8,128)}), f32[32,4096]{1,0:T(8,128)}) %reduce-scatter.18.cloned.1.call-update) | async-done | bytes 524304 | tf_op jit(solution)/shard_map/reduce_scatter | solution.py:283
  1115.6 1.8 multiply_reduce_fusion.3
  1118.1 184.3 %reduce-scatter.20.cloned.1.call-done = f32[128,1024]{1,0:T(8,128)} async-done(((f32[4096,1024]{1,0:T(8,128)}), f32[128,1024]{1,0:T(8,128)}) %reduce-scatter.20.cloned.1.call-update) | async-done | bytes 524304 | tf_op jit(solution)/shard_map/reduce_scatter | solution.py:284
  1305.5 5.9 fusion.23
  1311.4 36.9 %psum.7 = f32[]{:T(128)} all-reduce(f32[]{:T(128)S(6)} %add.341), channel_id=1, replica_groups=mesh['dp'=4,'seq'=8] {'dp','seq'}, use_global_device_ids=true, to_apply=%region_38.0 | all-reduce | flops 1 | bytes 8 | tf_op jit(solution)/shard_map/psum | solution.py:290
  1350.4 2.5 multiply_subtract_fusion.2
  (227 shorter events, 57.5 us)
Async XLA Ops:
  7.2 76.9 %all-gather.8.cloned.1.call-start = ((), (), s32[]{:S(2)}) async-start(), calls=%async_computation.7 | async-start | bytes 6488064 | tf_op jit(solution)/shard_map/all_gather | solution.py:152
  9.0 107.6 %all-gather.10.cloned.1.call-start = ((), (), s32[]{:S(2)}) async-start(), calls=%async_computation.8 | async-start | bytes 2359296 | tf_op jit(solution)/shard_map/all_gather | solution.py:175
  87.9 3.3 copy-start.28
  88.8 58.6 %all-gather.12.cloned.1.call-start = ((), (), s32[]{:S(2)}) async-start(), calls=%async_computation.9 | async-start | bytes 2359296 | tf_op jit(solution)/shard_map/all_gather | solution.py:174
  89.6 117.2 %all-gather.14.cloned.1.call-start = ((), (), s32[]{:S(2)}) async-start(), calls=%async_computation.10 | async-start | bytes 2162688 | tf_op jit(solution)/shard_map/all_gather | solution.py:153
  90.3 196.0 %all-gather.16.cloned.1.call-start = ((), (), s32[]{:S(2)}) async-start(), calls=%async_computation.11 | async-start | bytes 8650752 | tf_op jit(solution)/shard_map/all_gather | solution.py:154
  91.2 274.6 %all-gather.18.cloned.1.call-start = ((), (), s32[]{:S(2)}) async-start(), calls=%async_computation.12 | async-start | bytes 8650752 | tf_op jit(solution)/shard_map/all_gather | solution.py:155
  92.0 362.5 %reduce-scatter.24.cloned.1.call-start = ((), (), s32[]{:S(2)}) async-start(), calls=%async_computation.17 | async-start | bytes 2359296
  209.1 172.7 %copy-start.7 = (f32[128,1024]{1,0:T(8,128)}, f32[128,1024]{1,0:T(8,128)S(1)}, u32[]{:S(2)}) copy-start(f32[128,1024]{1,0:T(8,128)S(1)} %get-tuple-element.703) | copy-start | bytes 1572868
  365.8 6.9 slice-start
  365.8 5.5 copy-start.22
  365.8 6.9 slice-start.1
  371.6 7.1 slice-start.2
  372.7 5.9 copy-start.34
  372.7 5.9 slice-start.3
  378.7 3.1 copy-start.17
  382.1 3.1 copy-start.24
  382.2 3.0 copy-start.20
  392.1 2.8 copy-start
  397.2 2.9 copy-start.14
  404.6 2.8 copy-start
  407.4 2.5 copy-start.1
  410.0 2.9 copy-start.14
  420.0 71.3 %reduce-scatter.22.cloned.1.call-start = ((), (), s32[]{:S(2)}) async-start(), calls=%async_computation.16 | async-start | bytes 2359296
  424.1 32.8 %copy-start.16 = (f32[128,16,64]{0,2,1:T(8,128)S(1)}, f32[128,16,64]{0,2,1:T(8,128)}, u32[]{:S(2)}) copy-start(f32[128,16,64]{0,2,1:T(8,128)} %get-tuple-element.395) | copy-start | bytes 1572868
  424.2 32.8 %copy-start.21 = (bf16[128,1024]{1,0:T(8,128)(2,1)S(1)}, bf16[128,1024]{1,0:T(8,128)(2,1)}, u32[]{:S(2)}) copy-start(bf16[128,1024]{1,0:T(8,128)(2,1)} %copy-done.20) | copy-start | bytes 786436
  424.2 202.6 %reduce-scatter.28.cloned.1.call-start = ((), (), s32[]{:S(2)}) async-start(), calls=%async_computation.19 | async-start | bytes 540672
  456.9 311.0 %reduce-scatter.16.cloned.1.call-start = ((), (), s32[]{:S(2)}) async-start(), calls=%async_computation.13 | async-start | bytes 4325376 | tf_op jit(solution)/shard_map/reduce_scatter | solution.py:282
  459.7 32.7 %copy-start.19 = (bf16[1,128,1024]{2,1,0:T(8,128)(2,1)S(1)}, bf16[1,128,1024]{2,1,0:T(8,128)(2,1)}, u32[]{:S(2)}) copy-start(bf16[1,128,1024]{2,1,0:T(8,128)(2,1)} %param.23) | copy-start | bytes 786436
  459.7 468.0 %reduce-scatter.26.cloned.1.call-start = ((), (), s32[]{:S(2)}) async-start(), calls=%async_computation.18 | async-start | bytes 12976128 | tf_op jit(solution)/shard_map/reduce_scatter | solution.py:281
  511.3 604.3 %reduce-scatter.18.cloned.1.call-start = ((), (), s32[]{:S(2)}) async-start(), calls=%async_computation.14 | async-start | bytes 17301504 | tf_op jit(solution)/shard_map/reduce_scatter | solution.py:283
  520.9 781.4 %reduce-scatter.20.cloned.1.call-start = ((), (), s32[]{:S(2)}) async-start(), calls=%async_computation.15 | async-start | bytes 17301504 | tf_op jit(solution)/shard_map/reduce_scatter | solution.py:284
  769.5 535.9 %copy-start.25 = (f32[128,1024]{1,0:T(8,128)S(1)}, f32[128,1024]{1,0:T(8,128)}, u32[]{:S(2)}) copy-start(f32[128,1024]{1,0:T(8,128)} %copy-done.24) | copy-start | bytes 1572868
  1305.4 43.6 %copy-start.45 = (f32[32,12]{0,1:T(8,128)S(1)}, f32[32,12]{0,1:T(8,128)}, u32[]{:S(2)}) copy-start(f32[32,12]{0,1:T(8,128)} %param.29) | copy-start | bytes 4612
  1305.4 44.9 %copy-start.32 = (f32[32,3072]{1,0:T(8,128)S(1)}, f32[32,3072]{1,0:T(8,128)}, u32[]{:S(2)}) copy-start(f32[32,3072]{1,0:T(8,128)} %param.25) | copy-start | bytes 1179652
  1305.4 44.9 %copy-start.33 = (f32[32,3072]{1,0:T(8,128)S(1)}, f32[32,3072]{1,0:T(8,128)}, u32[]{:S(2)}) copy-start(f32[32,3072]{1,0:T(8,128)} %reduce-scatter.26.cloned.1.call-done) | copy-start | bytes 1179652
  1311.3 41.5 %copy-start.37 = (f32[32,1024]{1,0:T(8,128)S(1)}, f32[32,1024]{1,0:T(8,128)}, u32[]{:S(2)}) copy-start(f32[32,1024]{1,0:T(8,128)} %param.26) | copy-start | bytes 393220
  1311.3 41.5 %copy-start.38 = (f32[32,1024]{1,0:T(8,128)S(1)}, f32[32,1024]{1,0:T(8,128)}, u32[]{:S(2)}) copy-start(f32[32,1024]{1,0:T(8,128)} %reduce-scatter.16.cloned.1.call-done) | copy-start | bytes 393220
  1311.3 41.5 %copy-start.43 = (f32[32,1024]{1,0:T(8,128)S(1)}, f32[32,1024]{1,0:T(8,128)}, u32[]{:S(2)}) copy-start(f32[32,1024]{1,0:T(8,128)} %param.31) | copy-start | bytes 393220
  1311.3 41.5 %copy-start.44 = (f32[32,1024]{1,0:T(8,128)S(1)}, f32[32,1024]{1,0:T(8,128)}, u32[]{:S(2)}) copy-start(f32[32,1024]{1,0:T(8,128)} %param.36) | copy-start | bytes 393220
  1311.3 42.4 %copy-start.27 = (f32[32,4096]{1,0:T(8,128)S(1)}, f32[32,4096]{1,0:T(8,128)}, u32[]{:S(2)}) copy-start(f32[32,4096]{1,0:T(8,128)} %param.27) | copy-start | bytes 1572868
  1311.4 42.4 %copy-start.30 = (f32[32,4096]{1,0:T(8,128)S(1)}, f32[32,4096]{1,0:T(8,128)}, u32[]{:S(2)}) copy-start(f32[32,4096]{1,0:T(8,128)} %reduce-scatter.18.cloned.1.call-done) | copy-start | bytes 1572868
  1311.4 42.4 %copy-start.39 = (f32[32,4096]{1,0:T(8,128)S(1)}, f32[32,4096]{1,0:T(8,128)}, u32[]{:S(2)}) copy-start(f32[32,4096]{1,0:T(8,128)} %param.32) | copy-start | bytes 1572868
  1311.4 42.4 %copy-start.40 = (f32[32,4096]{1,0:T(8,128)S(1)}, f32[32,4096]{1,0:T(8,128)}, u32[]{:S(2)}) copy-start(f32[32,4096]{1,0:T(8,128)} %param.37) | copy-start | bytes 1572868
  1352.9 2.5 copy-start.29
  1352.9 2.5 copy-start.31
  1352.9 2.5 copy-start.41
  1352.9 2.5 copy-start.42
  (25 other events, 41.8 us)
Sparse Core Ops, SparseCore 0:
  11.6 72.4 all-gather.7
  88.9 27.5 all-gather.9
  118.7 28.5 all-gather.11
  150.8 55.9 all-gather.13
  210.2 76.1 all-gather.15
  289.8 75.9 all-gather.17
  420.1 34.3 reduce-scatter.23
  456.8 34.3 reduce-scatter.21
  494.1 132.6 reduce-scatter.27
  628.9 138.9 reduce-scatter.15
  775.0 152.6 reduce-scatter.25
  929.8 185.7 reduce-scatter.17
  1117.9 184.3 reduce-scatter.19
where the time goes:
time: 1370 us
  waiting for transfers between devices  1080 us (79%)
  matrix products  89.3 us (7%)
  blocking collectives  81 us (6%)
  local copies, waits for them, and re-layouts  61.6 us (4%)
  other arithmetic  28.5 us (2%)
  between operations  20.1 us (1%)
    reduce_scatter x1, waiting for transfers between devices, on_device(): lax.psum_scatter(grad_weight_down, ('dp', 'seq'), scatter_dimension=0, ti...  184 us
    reduce_scatter x1, waiting for transfers between devices, on_device(): lax.psum_scatter(grad_weight_up, ('dp', 'seq'), scatter_dimension=0, tile...  184 us
    reduce_scatter x1, waiting for transfers between devices, on_device(): lax.psum_scatter(grad_weight_qkv, ('dp', 'seq'), scatter_dimension=0, til...  158 us
    unnamed x16, waiting for transfers between devices  157 us
    reduce_scatter x1, waiting for transfers between devices, on_device(): lax.psum_scatter(grad_weight_out, ('dp', 'seq'), scatter_dimension=0, til...  140 us
    all_gather x1, waiting for transfers between devices, on_device(): lax.all_gather(weight_up.astype(jnp.bfloat16), ('dp', 'seq'), axis=0, til...  77 us
    all_gather x1, waiting for transfers between devices, on_device(): lax.all_gather(weight_down.astype(jnp.bfloat16), ('dp', 'seq'), axis=0, t...  69.7 us
    all_gather x1, blocking collectives, on_device(): lax.all_gather(small_params.astype(jnp.bfloat16), ('dp', 'seq'), axis=0,...  44.2 us
  transfers between devices with their start and end apart: 13, of which 13 were waited for; matrix products, arithmetic and copies ran while one was open for 7% of the time, Pallas kernels for 0%

commit v1 on v0

--- a/solution.py
+++ b/solution.py
@@ -1,6 +1,9 @@
 import jax
 import jax.numpy as jnp
 from jax import lax
+from jax.experimental import pallas as pl
+from jax.experimental.pallas import tpu as pltpu
+from jax.sharding import Mesh
 from jax.sharding import PartitionSpec as P
 
 HEAD = 64
@@ -186,12 +189,7 @@
     activation_low = activation.astype(jnp.bfloat16)
     downward = jnp.dot(activation_low, full_down, preferred_element_type=jnp.float32) + bias_down
     output, norm_two_back = jax.vjp(layer_norm, hidden + downward, gain_two, shift_two)
-    back_qkv, back_out, back_up, back_down = (
-        lax.all_gather(weight_qkv.astype(jnp.bfloat16), ("dp", "seq"), axis=0, tiled=True),
-        lax.all_gather(weight_out.astype(jnp.bfloat16), ("dp", "seq"), axis=0, tiled=True),
-        lax.all_gather(weight_up.astype(jnp.bfloat16), ("dp", "seq"), axis=0, tiled=True),
-        lax.all_gather(weight_down.astype(jnp.bfloat16), ("dp", "seq"), axis=0, tiled=True),
-    )
+    back_qkv, back_out, back_up, back_down = (full_qkv, full_out, full_up, full_down)
     grad_sum_two, grad_gain_two, grad_shift_two = norm_two_back(cotangent[0].astype(jnp.float32))
     grad_down_low = grad_sum_two.astype(jnp.bfloat16)
     grad_bias_down = jnp.sum(grad_down_low.astype(jnp.float32), axis=0)
@@ -327,46 +325,426 @@
     )
 
 
+AXES = ("y", "x", "h", "l", "c")
+LOW = jnp.bfloat16
+WIDE = jnp.float32
+
+
+def swap(value, axes):
+    axes = tuple(name for name in AXES if name in axes)
+    last = 2 ** len(axes) - 1
+    return lax.ppermute(value, axes, [(i, i ^ last) for i in range(last + 1)])
+
+
+def bit(name):
+    return lax.axis_index(name)
+
+
+def gather_square(value, a, b):
+    half = value.shape[0] // 2
+    from_a, from_b = swap(value, (a,)), swap(value, (b,))
+    low_half = swap(from_a[:half], (b,))
+    high_half = swap(from_b[half:], (a,))
+    return [value, from_b, from_a, jnp.concatenate([low_half, high_half], axis=0)]
+
+
+def gather_direct(value, a, b):
+    return [value, swap(value, (b,)), swap(value, (a,)), swap(value, (a, b))]
+
+
+def exchange_direct(parts, a, b):
+    return [parts[0], swap(parts[1], (b,)), swap(parts[2], (a,)), swap(parts[3], (a, b))]
+
+
+def scatter_square(parts, a, b):
+    own, to_b, to_a, to_far = parts
+    half = own.shape[0] // 2
+    first = swap(to_far[:half].astype(LOW), (a,))
+    second = swap(to_far[half:].astype(LOW), (b,))
+    to_b = jnp.concatenate([to_b[:half] + first.astype(WIDE), to_b[half:]], axis=0)
+    to_a = jnp.concatenate([to_a[:half], to_a[half:] + second.astype(WIDE)], axis=0)
+    from_b = swap(to_b.astype(LOW), (b,))
+    from_a = swap(to_a.astype(LOW), (a,))
+    return own + from_b.astype(WIDE) + from_a.astype(WIDE)
+
+
+def place(blocks, position, axis=0):
+    size = blocks[0].shape[axis]
+    shape = list(blocks[0].shape)
+    shape[axis] = size * len(blocks)
+    result = jnp.zeros(shape, blocks[0].dtype)
+    for index, block in enumerate(blocks):
+        result = lax.dynamic_update_slice_in_dim(result, block, (position ^ index) * size, axis)
+    return result
+
+
+def pick(value, position, count, axis=0):
+    size = value.shape[axis] // count
+    return [
+        lax.dynamic_slice_in_dim(value, (position ^ index) * size, size, axis)
+        for index in range(count)
+    ]
+
+
+def head_masks(shape, axis):
+    lane = lax.broadcasted_iota(jnp.int32, shape, axis)
+    return [lane < HEAD, lane >= HEAD]
+
+
+def forward_kernel(q_ref, k_ref, v_ref, o_ref, lse_ref):
+    queries, keys, values = q_ref[...], k_ref[...], v_ref[...]
+    lanes = head_masks(queries.shape, 1)
+    values_t = values.T
+    zero = jnp.zeros_like(queries)
+    outs = []
+    for head in range(2):
+        query = jnp.where(lanes[head], queries, zero)
+        scores = against(keys, query) * SCORE_SCALE
+        top = jnp.max(scores, axis=0, keepdims=True)
+        weights = jnp.exp(scores - top)
+        total = jnp.sum(weights, axis=0, keepdims=True)
+        probs = (weights * (1.0 / total)).astype(LOW)
+        lse_ref[head : head + 1, :] = top + jnp.log(total)
+        outs.append(jnp.dot(values_t, probs, preferred_element_type=WIDE))
+    rows = head_masks(outs[0].shape, 0)
+    o_ref[...] = jnp.where(rows[0], outs[0], outs[1]).T.astype(LOW)
+
+
+def attention(queries, keys, values, block=256):
+    length, width = queries.shape
+    whole = pl.BlockSpec((length, width), lambda i: (0, 0))
+    part = pl.BlockSpec((block, width), lambda i: (i, 0))
+    return pl.pallas_call(
+        forward_kernel,
+        grid=(length // block,),
+        in_specs=[part, whole, whole],
+        out_specs=[part, pl.BlockSpec((2, block), lambda i: (0, i))],
+        out_shape=[
+            jax.ShapeDtypeStruct((length, width), LOW),
+            jax.ShapeDtypeStruct((2, length), WIDE),
+        ],
+        compiler_params=pltpu.CompilerParams(vmem_limit_bytes=40 * 2**20),
+        cost_estimate=pl.CostEstimate(
+            flops=16 * length * length * width, bytes_accessed=2**20, transcendentals=2 * length * length
+        ),
+    )(queries, keys, values)
+
+
+def backward_kernel(q_ref, do_ref, k_ref, v_ref, lse_ref, dq_ref, dk_ref, dv_ref, dk_sum, dv_sum):
+    step = pl.program_id(0)
+    queries, douts, keys, values = q_ref[...], do_ref[...], k_ref[...], v_ref[...]
+    lanes = head_masks(queries.shape, 1)
+    keys_t = keys.T
+    zero = jnp.zeros_like(queries)
+    all_probs, all_grads, all_query, all_dout, outs = [], [], [], [], []
+    for head in range(2):
+        query = jnp.where(lanes[head], queries, zero)
+        dout = jnp.where(lanes[head], douts, zero)
+        scores = against(keys, query) * SCORE_SCALE
+        probs = jnp.exp(scores - lse_ref[head : head + 1, :])
+        grad_probs = against(values, dout)
+        delta = jnp.sum(probs * grad_probs, axis=0, keepdims=True)
+        grads = (probs * (grad_probs - delta)).astype(LOW)
+        all_probs.append(probs.astype(LOW))
+        all_grads.append(grads)
+        all_query.append(query)
+        all_dout.append(dout)
+        outs.append(jnp.dot(keys_t, grads, preferred_element_type=WIDE))
+    rows = head_masks(outs[0].shape, 0)
+    dq_ref[...] = (jnp.where(rows[0], outs[0], outs[1]) * SCORE_SCALE).T.astype(LOW)
+    part_keys = jnp.dot(
+        jnp.concatenate(all_grads, axis=1),
+        jnp.concatenate(all_query, axis=0),
+        preferred_element_type=WIDE,
+    )
+    part_values = jnp.dot(
+        jnp.concatenate(all_probs, axis=1),
+        jnp.concatenate(all_dout, axis=0),
+        preferred_element_type=WIDE,
+    )
+
+    @pl.when(step == 0)
+    def _():
+        dk_sum[...] = part_keys
+        dv_sum[...] = part_values
+
+    @pl.when(step > 0)
+    def _():
+        dk_sum[...] += part_keys
+        dv_sum[...] += part_values
+
+    @pl.when(step == pl.num_programs(0) - 1)
+    def _():
+        dk_ref[...] = (dk_sum[...] * SCORE_SCALE).astype(LOW)
+        dv_ref[...] = dv_sum[...].astype(LOW)
+
+
+def attention_back(queries, douts, keys, values, lse, block=256):
+    length, width = queries.shape
+    whole = pl.BlockSpec((length, width), lambda i: (0, 0))
+    part = pl.BlockSpec((block, width), lambda i: (i, 0))
+    return pl.pallas_call(
+        backward_kernel,
+        grid=(length // block,),
+        in_specs=[part, part, whole, whole, pl.BlockSpec((2, block), lambda i: (0, i))],
+        out_specs=[part, whole, whole],
+        out_shape=[jax.ShapeDtypeStruct((length, width), LOW)] * 3,
+        scratch_shapes=[pltpu.VMEM((length, width), WIDE)] * 2,
+        compiler_params=pltpu.CompilerParams(vmem_limit_bytes=40 * 2**20),
+        cost_estimate=pl.CostEstimate(
+            flops=40 * length * length * width, bytes_accessed=2**21, transcendentals=2 * length * length
+        ),
+    )(queries, douts, keys, values, lse)
+
+
+def on_square(
+    tokens,
+    cotangent,
+    weight_qkv,
+    weight_out,
+    weight_up,
+    weight_down,
+    small_params,
+    moment_qkv,
+    moment_out,
+    moment_up,
+    moment_down,
+    moment_small,
+    second_qkv,
+    second_out,
+    second_up,
+    second_down,
+    second_small,
+):
+    rows = tokens[0]
+    count, width = rows.shape
+    own = weight_qkv.shape[0]
+    ratio = weight_up.shape[1] // width
+    columns = small_params.shape[1]
+    part = width // 8
+    units = weight_up.shape[1] // 8
+    iy, ix, ih, il, ic = (bit(name) for name in AXES)
+    at_seq = 4 * ih + 2 * il + ic
+    at_z = 2 * ih + il
+    at_dp = 2 * iy + ix
+    at_yh = 2 * iy + ih
+
+    mine = gather_direct(rows, "h", "l")
+    lead = jnp.concatenate(mine, axis=0)
+    tokens_all = jnp.concatenate([lead, swap(lead, ("c",))], axis=0)
+
+    low_qkv = weight_qkv.astype(LOW).reshape(own, 3, 8, part).transpose(2, 0, 1, 3)
+    low_qkv = low_qkv.reshape(8, own, 3 * part)
+    low_small = small_params.astype(LOW).reshape(1, 1, own * columns)
+    low_small = jnp.broadcast_to(low_small, (8, 8, own * columns))
+    packed = jnp.concatenate([low_qkv, low_small], axis=1)
+    packed = lax.all_to_all(packed, ("h", "l", "c"), 0, 0, tiled=True)
+    packed = place(gather_square(packed, "y", "x"), at_dp)
+    full_qkv = packed[:, :own].reshape(width, 3 * part)
+    table = packed[:, own].astype(WIDE).reshape(width, columns)
+    (
+        bias_query,
+        bias_value,
+        bias_out,
+        bias_up,
+        bias_down,
+        gain_one,
+        shift_one,
+        gain_two,
+        shift_two,
+    ) = unpack(table)
+
+    full_out = lax.all_gather(weight_out.astype(LOW), AXES, axis=0, tiled=True)
+
+    low_up = weight_up.astype(LOW).reshape(own, 2, 2, 2, 4, units // 4)
+    low_up = low_up.transpose(2, 4, 0, 1, 3, 5).reshape(8, own, units)
+    low_up = lax.all_to_all(low_up, ("x", "l", "c"), 0, 0, tiled=True)
+    up_blocks = gather_square(low_up, "y", "h")
+    full_up = jnp.zeros((2, 2, 2, 4 * own, units), LOW)
+    for index, block in enumerate(up_blocks):
+        block = block.reshape(1, 2, 1, 4 * own, units)
+        full_up = lax.dynamic_update_slice(
+            full_up, block, (iy ^ (index // 2), 0, ih ^ (index % 2), 0, 0)
+        )
+    full_up = full_up.reshape(width, units)
+    full_down = place(gather_square(weight_down.astype(LOW), "y", "h"), at_yh)
+
+    take = lambda vector: lax.dynamic_slice_in_dim(vector, at_seq * part, part)
+    projected = jnp.dot(tokens_all, full_qkv, preferred_element_type=WIDE)
+    query = (projected[:, :part] + take(bias_query)).astype(LOW)
+    keys = projected[:, part : 2 * part].astype(LOW)
+    values = (projected[:, 2 * part :] + take(bias_value)).astype(LOW)
+    attended_mine, lse = attention(query, keys, values)
+
+    near, far = attended_mine[: 4 * count], attended_mine[4 * count :]
+    far = swap(far, ("c",))
+    both = place([near, far], ic, axis=1).reshape(4, count, 2 * part)
+    sources = exchange_direct([both[0], both[1], both[2], both[3]], "h", "l")
+    attended = place(sources, at_z, axis=1)
+
+    branch = jnp.dot(attended, full_out, preferred_element_type=WIDE) + bias_out
+    middle = rows.astype(WIDE) + branch
+    hidden, norm_one_back = jax.vjp(layer_norm, middle, gain_one, shift_one)
+
+    def gather_group(value):
+        lead = jnp.concatenate(gather_square(value, "x", "l"), axis=0)
+        return jnp.concatenate([lead, swap(lead, ("c",))], axis=0)
+
+    def scatter_group(partial):
+        near = partial[: 4 * count] + swap(partial[4 * count :].astype(LOW), ("c",)).astype(WIDE)
+        return scatter_square([near[i * count : (i + 1) * count] for i in range(4)], "x", "l")
+
+    hidden_all = gather_group(hidden.astype(LOW))
+    bias_units = bias_up.reshape(2, 2, 2, 4, units // 4)
+    bias_units = lax.dynamic_slice(
+        bias_units, (0, ix, 0, 2 * il + ic, 0), (2, 1, 2, 1, units // 4)
+    ).reshape(units)
+    upward = jnp.dot(hidden_all, full_up, preferred_element_type=WIDE) + bias_units
+    activation, gelu_back = jax.vjp(exact_gelu, upward)
+    activation_low = activation.astype(LOW)
+    downward = scatter_group(jnp.dot(activation_low, full_down, preferred_element_type=WIDE))
+    output, norm_two_back = jax.vjp(
+        layer_norm, hidden + (downward + bias_down), gain_two, shift_two
+    )
+
+    grad_sum_two, grad_gain_two, grad_shift_two = norm_two_back(cotangent[0].astype(WIDE))
+    grad_down_low = grad_sum_two.astype(LOW)
+    grad_bias_down = jnp.sum(grad_down_low.astype(WIDE), axis=0)
+    grad_down_all = gather_group(grad_down_low)
+    grad_activation = against(grad_down_all, full_down)
+    grad_up_low = gelu_back(grad_activation)[0].astype(LOW)
+    grad_hidden = grad_sum_two + scatter_group(against(grad_up_low, full_up))
+    part_down = cross(activation_low, grad_down_all)
+    part_up = cross(hidden_all, grad_up_low)
+    grad_bias_up = jnp.sum(grad_up_low.astype(WIDE), axis=0)
+    owned_down = scatter_square(pick(part_down, at_yh, 4), "y", "h")
+    part_up = part_up.reshape(2, 2, 2, 4 * own, units)
+    up_parts = [
+        lax.dynamic_slice(
+            part_up, (iy ^ (i // 2), 0, ih ^ (i % 2), 0, 0), (1, 2, 1, 4 * own, units)
+        ).reshape(8 * own, units)
+        for i in range(4)
+    ]
+    owned_up = scatter_square(up_parts, "y", "h").astype(LOW).reshape(8, own, units)
+    owned_up = lax.all_to_all(owned_up, ("x", "l", "c"), 0, 0, tiled=True)
+    owned_up = owned_up.reshape(2, 4, own, 2, 2, units // 4).transpose(2, 3, 0, 4, 1, 5)
+    owned_up = owned_up.reshape(own, 8 * units).astype(WIDE)
+
+    grad_middle, grad_gain_one, grad_shift_one = norm_one_back(grad_hidden)
+    grad_branch_low = grad_middle.astype(LOW)
+    grad_bias_out = jnp.sum(grad_branch_low.astype(WIDE), axis=0)
+    grad_attended = against(grad_branch_low, full_out).astype(LOW)
+    sources = exchange_direct(pick(grad_attended, at_z, 4, axis=1), "h", "l")
+    both = jnp.concatenate(sources, axis=0)
+    near, far = pick(both, ic, 2, axis=1)
+    dout = jnp.concatenate([near, swap(far, ("c",))], axis=0)
+
+    grad_query, grad_keys, grad_values = attention_back(query, dout, keys, values, lse)
+    grad_projected = jnp.concatenate([grad_query, grad_keys, grad_values], axis=1)
+    part_qkv = cross(tokens_all, grad_projected)
+    owned_qkv = scatter_square(pick(part_qkv, at_dp, 4), "y", "x")
+    owned_qkv = owned_qkv.astype(LOW).reshape(8, own, 3 * part)
+    owned_qkv = lax.all_to_all(owned_qkv, ("h", "l", "c"), 0, 0, tiled=True)
+    owned_qkv = owned_qkv.reshape(8, own, 3, part).transpose(1, 2, 0, 3)
+    owned_qkv = owned_qkv.reshape(own, 3 * width).astype(WIDE)
+
+    part_out = cross(attended, grad_branch_low).reshape(16, 2, own, width)
+    out_near, out_far = pick(part_out, ic, 2, axis=1)
+    out_near = out_near + swap(out_far.astype(LOW), ("c",)).astype(WIDE)
+    out_near = scatter_square(pick(out_near.reshape(16 * own, width), at_dp, 4), "y", "x")
+    pieces = exchange_direct(
+        [piece.astype(LOW) for piece in pick(out_near, at_z, 4)], "h", "l"
+    )
+    owned_out = sum(piece.astype(WIDE) for piece in pieces)
+
+    part_rows = against(grad_projected, full_qkv)
+    near = part_rows[: 4 * count] + swap(part_rows[4 * count :].astype(LOW), ("c",)).astype(WIDE)
+    near = near.astype(LOW)
+    pieces = exchange_direct([near[i * count : (i + 1) * count] for i in range(4)], "h", "l")
+    grad_rows = grad_middle + sum(piece.astype(WIDE) for piece in pieces)
+
+    blank = jnp.zeros((width,), WIDE)
+    put = lambda vector: lax.dynamic_update_slice_in_dim(blank, vector, at_seq * part, 0)
+    row_query = put(jnp.sum(grad_query.astype(WIDE), axis=0))
+    row_value = put(jnp.sum(grad_values.astype(WIDE), axis=0))
+    rows_up = lax.dynamic_update_slice(
+        jnp.zeros((2, 2, 2, 4, units // 4), WIDE),
+        grad_bias_up.reshape(2, 1, 2, 1, units // 4),
+        (0, ix, 0, 2 * il + ic, 0),
+    ).reshape(ratio, width)
+    small = jnp.concatenate(
+        [
+            jnp.stack([row_query, row_value, grad_bias_out]),
+            rows_up,
+            jnp.stack([grad_bias_down, grad_gain_one, grad_shift_one, grad_gain_two, grad_shift_two]),
+        ]
+    )
+    for name in ("c", "x", "y", "l", "h"):
+        small = small + swap(small, (name,))
+    at_all = 8 * at_dp + at_seq
+    owned_small = lax.dynamic_slice_in_dim(small, at_all * own, own, axis=1).T
+
+    squares = jnp.sum(owned_qkv * owned_qkv) + jnp.sum(owned_out * owned_out)
+    squares = squares + jnp.sum(owned_up * owned_up) + jnp.sum(owned_down * owned_down)
+    squares = squares + jnp.sum(owned_small * owned_small)
+    total = jnp.broadcast_to(squares, (8, 128))
+    for name in ("c", "x", "y", "l", "h"):
+        total = total + swap(total, (name,))
+    grad_norm = jnp.sqrt(total[0, 0])
+    factor = jnp.minimum(1.0, CLIP_LIMIT / (grad_norm + 1e-06))
+    new_qkv, new_moment_qkv, new_second_qkv = adam_update(
+        weight_qkv, owned_qkv * factor, moment_qkv, second_qkv, RATE_MATRIX, WEIGHT_DECAY
+    )
+    new_out, new_moment_out, new_second_out = adam_update(
+        weight_out, owned_out * factor, moment_out, second_out, RATE_OUTPUT, WEIGHT_DECAY
+    )
+    new_up, new_moment_up, new_second_up = adam_update(
+        weight_up, owned_up * factor, moment_up, second_up, RATE_MATRIX, WEIGHT_DECAY
+    )
+    new_down, new_moment_down, new_second_down = adam_update(
+        weight_down, owned_down * factor, moment_down, second_down, RATE_MATRIX, WEIGHT_DECAY
+    )
+    new_small, new_moment_small, new_second_small = adam_update(
+        small_params, owned_small * factor, moment_small, second_small, RATE_SMALL, 0.0
+    )
+    return (
+        output.astype(jnp.bfloat16)[None],
+        grad_rows[None],
+        grad_norm,
+        new_qkv,
+        new_out,
+        new_up,
+        new_down,
+        new_small,
+        new_moment_qkv,
+        new_moment_out,
+        new_moment_up,
+        new_moment_down,
+        new_moment_small,
+        new_second_qkv,
+        new_second_out,
+        new_second_up,
+        new_second_down,
+        new_second_small,
+    )
+
+
 def solution(mesh):
-    in_specs = (
-        P("dp", "seq", None),
-        P("dp", "seq", None),
-        P(("dp", "seq"), None),
-        P(("dp", "seq"), None),
-        P(("dp", "seq"), None),
-        P(("dp", "seq"), None),
-        P(("dp", "seq"), None),
-        P(("dp", "seq"), None),
-        P(("dp", "seq"), None),
-        P(("dp", "seq"), None),
-        P(("dp", "seq"), None),
-        P(("dp", "seq"), None),
-        P(("dp", "seq"), None),
-        P(("dp", "seq"), None),
-        P(("dp", "seq"), None),
-        P(("dp", "seq"), None),
-        P(("dp", "seq"), None),
-    )
-    out_specs = (
-        P("dp", "seq", None),
-        P("dp", "seq", None),
-        P(),
-        P(("dp", "seq"), None),
-        P(("dp", "seq"), None),
-        P(("dp", "seq"), None),
-        P(("dp", "seq"), None),
-        P(("dp", "seq"), None),
-        P(("dp", "seq"), None),
-        P(("dp", "seq"), None),
-        P(("dp", "seq"), None),
-        P(("dp", "seq"), None),
-        P(("dp", "seq"), None),
-        P(("dp", "seq"), None),
-        P(("dp", "seq"), None),
-        P(("dp", "seq"), None),
-        P(("dp", "seq"), None),
-        P(("dp", "seq"), None),
-    )
+    sizes = (mesh.shape["dp"], mesh.shape["seq"])
+    if sizes == (4, 8):
+        squares = Mesh(mesh.devices.reshape(2, 2, 2, 2, 2), AXES)
+        dp, seq = ("y", "x"), ("h", "l", "c")
+        body, mesh = on_square, squares
+        every = P(AXES, None)
+        over = P(dp, seq, None)
+    else:
+        body = on_device
+        every = P(("dp", "seq"), None)
+        over = P("dp", "seq", None)
     return jax.shard_map(
-        on_device, mesh=mesh, in_specs=in_specs, out_specs=out_specs, check_vma=False
-    )
+        body,
+        mesh=mesh,
+        in_specs=(over,) * 2 + (every,) * 15,
+        out_specs=(over,) * 2 + (P(),) + (every,) * 15,
+        check_vma=False,
+    )

time: 1370 us -> 393 us (0.29)
  waiting for transfers between devices: 1080 us -> 116 us
  starting transfers between devices: 0.79 us -> 117 us
  blocking collectives: 81 us -> 0 us
  matrix products: 89.3 us -> 35 us
  local copies, waits for them, and re-layouts: 61.6 us -> 37.4 us
  Pallas kernels: 0 us -> 15.9 us
  other arithmetic: 28.5 us -> 42.7 us
    reduce_scatter x4 -> x0, waiting for transfers between devices: 666 us -> none  [the longest x1 184 us: on_device(): lax.psum_scatter(grad_weight_down, ('dp', 'seq'), scatter_dimension=0, ti...]
    all_gather x6 -> x1, waiting for transfers between devices: 260 us -> 0.02 us  [on_square(): full_out = lax.all_gather(weight_out.astype(LOW), AXES, axis=0, tiled=True)]
    unnamed x16 -> x1, waiting for transfers between devices: 157 us -> 0.02 us
    ppermute x0 -> x78, waiting for transfers between devices: none -> 108 us  [swap(): return lax.ppermute(value, axes, [(i, i ^ last) for i in range(last + 1)])]
    ppermute x0 -> x78, starting transfers between devices: none -> 98.8 us  [swap(): return lax.ppermute(value, axes, [(i, i ^ last) for i in range(last + 1)])]
    all_gather x1 -> x0, blocking collectives: 44.2 us -> none  [on_device(): lax.all_gather(small_params.astype(jnp.bfloat16), ('dp', 'seq'), axis=0,...]
    psum x1 -> x0, blocking collectives: 36.9 us -> none  [on_device(): total = lax.psum(squares, ('dp', 'seq'))]
    dot_general x18 -> x4, matrix products: 47.7 us -> 16.6 us  [the longest x1 8.71 us: on_square(): jnp.dot(hidden_all, full_up, preferred_element_type=WIDE) + bias_units]
  transfers between devices with their start and end apart: 13 -> 83, of which waited for: 13 -> 39; matrix products, arithmetic and copies ran while one was open for 7% -> 19% of each run, Pallas kernels for 0% -> 4%
where the time goes in v1:
time: 393 us; the launch traced here: 386 us
  starting transfers between devices  117 us (30%)
  waiting for transfers between devices  116 us (30%)
  other arithmetic  42.7 us (11%)
  local copies, waits for them, and re-layouts  37.4 us (10%)
  matrix products  35 us (9%)
  between operations  21 us (5%)
  Pallas kernels  15.9 us (4%)
    ppermute x78, waiting for transfers between devices, swap(): return lax.ppermute(value, axes, [(i, i ^ last) for i in range(last + 1)])  108 us
    ppermute x78, starting transfers between devices, swap(): return lax.ppermute(value, axes, [(i, i ^ last) for i in range(last + 1)])  98.8 us
    dot_general x4, matrix products, cross(): lax.dot_general(left, right, (((0,), (0,)), ((), ())), preferred_element_...  9.75 us
    unnamed x119, local copies, waits for them, and re-layouts  9.68 us
    dot_general x1, matrix products, on_square(): jnp.dot(hidden_all, full_up, preferred_element_type=WIDE) + bias_units  8.71 us
    pallas_call x1, Pallas kernels, attention_back(): pl.pallas_call(backward_kernel, grid=(length // block,), in_specs=[part,...  8.63 us
    dot_general x4, matrix products, against(): lax.dot_general(left, right, (((1,), (1,)), ((), ())), preferred_element_...  8.62 us
  transfers between devices with their start and end apart: 83, of which 39 were waited for; matrix products, arithmetic and copies ran while one was open for 19% of the time, Pallas kernels for 4%

profile of v1, /device:TPU:0, one launch (start us, length us, event | category | flops | bytes accessed | tf_op | source)
XLA Modules:
  0.0 385.6 jit_solution(3214703772301718499)
XLA Ops:
  7.3 3.1 collective-permute-start
  10.3 2.6 collective-permute-start.1
  16.8 5.1 %all-to-all-start = ((bf16[8,40,384]{2,1,0:T(8,128)(2,1)}), bf16[8,40,384]{2,1,0:T(8,128)(2,1)S(1)}, u32[]{:S(2)}, u32[]{:S(2)}) async-start(bf16[8,40,384]{2,1,0:T(8,128)(2,1)} %pad_maximum_fusion.14), calls=%async_computation | async-start | bytes 491520 | tf_op jit(solution)/shard_map/all_to_all | solution.py:541
  22.7 12.9 %collective-permute-done.1 = bf16[128,1024]{1,0:T(8,128)(2,1)S(1)} collective-permute-done((bf16[128,1024]{1,0:T(8,128)(2,1)}, bf16[128,1024]{1,0:T(8,128)(2,1)S(1)}, u32[]{:S(2)}, u32[]{:S(2)}) %collective-permute-start.1) | collective-permute-done | bytes 262176 | tf_op jit(solution)/shard_map/ppermute | solution.py:336
  37.3 5.5 %all-to-all-done = bf16[8,40,384]{2,1,0:T(8,128)(2,1)S(1)} async-done(((bf16[8,40,384]{2,1,0:T(8,128)(2,1)}), bf16[8,40,384]{2,1,0:T(8,128)(2,1)S(1)}, u32[]{:S(2)}, u32[]{:S(2)}) %all-to-all-start) | async-done | bytes 245792 | tf_op jit(solution)/shard_map/all_to_all | solution.py:541
  47.4 4.5 %collective-permute-done.5 = bf16[8,40,384]{2,1,0:T(8,128)(2,1)S(1)} collective-permute-done((bf16[8,40,384]{2,1,0:T(8,128)(2,1)S(1)}, bf16[8,40,384]{2,1,0:T(8,128)(2,1)S(1)}, u32[]{:S(2)}, u32[]{:S(2)}) %collective-permute-start.5) | collective-permute-done | bytes 245792 | tf_op jit(solution)/shard_map/ppermute | solution.py:336
  54.2 2.7 collective-permute-done.6
  58.8 2.4 slice_reduce_fusion.1
  62.4 2.8 fusion.76
  65.4 7.3 %shard_map.304 = (bf16[1024,128]{1,0:T(8,128)(2,1)S(1)}, f32[2,1024]{1,0:T(2,128)S(1)}) custom-call(bf16[1024,128]{1,0:T(8,128)(2,1)S(1)} %get-tuple-element.99.q_ref, bf16[1024,128]{1,0:T(8,128)(2,1)S(1)} %slice.501.k_ref, bf16[1024,128]{1,0:T(8,128)(2,1)S(1)} %get-tuple-element.98.v_ref), custom_call_target="tpu_custom_call" | custom-call | flops 2147483648 | bytes 1048576 | tf_op jit(solution)/shard_map/pallas_call | solution.py:417
  74.8 2.9 collective-permute-start.21
  81.3 4.6 %all-to-all-start.1 = ((bf16[8,32,512]{2,1,0:T(8,128)(2,1)}), bf16[8,32,512]{2,1,0:T(8,128)(2,1)}, u32[]{:S(2)}, u32[]{:S(2)}) async-start(bf16[8,32,512]{2,1,0:T(8,128)(2,1)} %reshape.229), calls=%async_computation.1 | async-start | bytes 524288 | tf_op jit(solution)/shard_map/all_to_all | solution.py:561
  92.3 2.5 collective-permute-start.11
  95.7 5.5 %collective-permute-done.10 = bf16[128,256]{1,0:T(8,128)(2,1)S(1)} collective-permute-done((bf16[128,256]{1,0:T(8,128)(2,1)S(1)}, bf16[128,256]{1,0:T(8,128)(2,1)S(1)}, u32[]{:S(2)}, u32[]{:S(2)}) %collective-permute-start.10) | collective-permute-done | bytes 65568 | tf_op jit(solution)/shard_map/ppermute | solution.py:336
  110.7 2.8 collective-permute-done.13
  113.8 3.7 collective-permute-start.15
  126.8 3.8 collective-permute-start.19
  134.7 2.9 collective-permute-done.19
  140.4 8.7 %multiply_convert_fusion = (bf16[1024,512]{1,0:T(8,128)(2,1)S(1)}, f32[1024,512]{1,0:T(8,128)}, f32[1024,512]{1,0:T(8,128)}) fusion(f32[512]{0:T(512)S(1)} %bitcast.170, bf16[1024,1024]{1,0:T(8,128)(2,1)} %constant_dynamic-update-slice_fusion.10, bf16[1024,512]{1,0:T(8,128)(2,1)} %bitcast.12), kind=kOutput, calls=%fused_computation.13 | convolution fusion | flops 1108344832 | bytes 8390656 | tf_op jit(solution)/shard_map/dot_general | solution.py:602
  149.1 2.9 fusion.77
  152.2 2.6 collective-permute-done.25
  158.5 2.6 collective-permute-done.26
  165.4 4.3 %collective-permute-done.27 = bf16[128,1024]{1,0:T(8,128)(2,1)S(1)} collective-permute-done((bf16[128,1024]{1,0:T(8,128)(2,1)S(1)}, bf16[128,1024]{1,0:T(8,128)(2,1)S(1)}, u32[]{:S(2)}, u32[]{:S(2)}) %collective-permute-start.27) | collective-permute-done | bytes 262176 | tf_op jit(solution)/shard_map/ppermute | solution.py:336
  176.6 3.5 collective-permute-done.31
  188.8 2.8 collective-permute-done.34
  192.7 3.3 fusion.83
  196.0 3.9 %convert_reduce_fusion = (f32[512]{0:T(512)S(1)}, bf16[1024,512]{1,0:T(8,128)(2,1)S(1)}) fusion(f32[1024,512]{1,0:T(8,128)S(1)} %copy-done.50, f32[1024,512]{1,0:T(8,128)S(1)} %copy-done.51, f32[512]{0:T(512)S(1)} %bitcast.171, bf16[1024,1024]{1,0:T(8,128)(2,1)} %constant_dynamic-update-slice_fusion.21, bf16[512,1024]{1,0:T(8,128)(2,1)} %maximum_dynamic-update-slice_fusion), kind=kOutput, calls=%fused_computation.9 | convolution fusion | flops 1082654208 | bytes 8392704 | tf_op jit(solution)/shard_map/dot_general | solution.py:60
  199.9 2.7 fusion.78
  202.6 2.8 fusion.82
  213.1 6.2 %collective-permute-done.66 = bf16[64,1024]{1,0:T(8,128)(2,1)S(1)} collective-permute-done((bf16[64,1024]{1,0:T(8,128)(2,1)S(1)}, bf16[64,1024]{1,0:T(8,128)(2,1)S(1)}, u32[]{:S(2)}, u32[]{:S(2)}) %collective-permute-start.66) | collective-permute-done | bytes 131104 | tf_op jit(solution)/shard_map/ppermute | solution.py:336
  225.2 4.0 %collective-permute-start.38 = (bf16[64,1024]{1,0:T(8,128)(2,1)S(1)}, bf16[64,1024]{1,0:T(8,128)(2,1)S(1)}, u32[]{:S(2)}, u32[]{:S(2)}) collective-permute-start(bf16[64,1024]{1,0:T(8,128)(2,1)S(1)} %get-tuple-element.106), channel_id=1, source_target_pairs={{0,2},{2,0},{1,3},{3,1},{4,6},{6,4},{5,7},{7,5},{8,10},{10,8},{9,1... | collective-permute-start | bytes 393224 | tf_op jit(solution)/shard_map/ppermute | solution.py:336
  229.5 7.2 %collective-permute-start.63 = (bf16[256,512]{1,0:T(8,128)(2,1)S(1)}, bf16[256,512]{1,0:T(8,128)(2,1)S(1)}, u32[]{:S(2)}, u32[]{:S(2)}) collective-permute-start(bf16[256,512]{1,0:T(8,128)(2,1)S(1)} %pad_maximum_fusion.11), channel_id=1, source_target_pairs={{0,16},{16,0},{1,17},{17,1},{2,18},{18,2},{3,19},{19,3},{4,20},{20... | collective-permute-start | bytes 786440 | tf_op jit(solution)/shard_map/ppermute | solution.py:336
  238.1 6.5 %collective-permute-done.61 = bf16[256,512]{1,0:T(8,128)(2,1)S(1)} collective-permute-done((bf16[256,512]{1,0:T(8,128)(2,1)S(1)}, bf16[256,512]{1,0:T(8,128)(2,1)S(1)}, u32[]{:S(2)}, u32[]{:S(2)}) %collective-permute-start.61) | collective-permute-done | bytes 262176 | tf_op jit(solution)/shard_map/ppermute | solution.py:336
  247.2 4.3 %all-to-all-start.3 = ((bf16[8,32,512]{2,1,0:T(8,128)(2,1)}), bf16[8,32,512]{2,1,0:T(8,128)(2,1)}, u32[]{:S(2)}, u32[]{:S(2)}) async-start(bf16[8,32,512]{2,1,0:T(8,128)(2,1)} %bitcast.157), calls=%async_computation.3 | async-start | bytes 524288 | tf_op jit(solution)/shard_map/all_to_all | solution.py:629
  251.5 2.5 multiply_reduce_fusion.1
  262.5 4.3 %collective-permute-done.41 = bf16[128,256]{1,0:T(8,128)(2,1)S(1)} collective-permute-done((bf16[128,256]{1,0:T(8,128)(2,1)S(1)}, bf16[128,256]{1,0:T(8,128)(2,1)S(1)}, u32[]{:S(2)}, u32[]{:S(2)}) %collective-permute-start.41) | collective-permute-done | bytes 65568 | tf_op jit(solution)/shard_map/ppermute | solution.py:336
  268.3 8.6 %shard_map.305 = (bf16[1024,128]{1,0:T(8,128)(2,1)S(1)}, bf16[1024,128]{1,0:T(8,128)(2,1)S(1)}, bf16[1024,128]{1,0:T(8,128)(2,1)S(1)}) custom-call(bf16[1024,128]{1,0:T(8,128)(2,1)S(1)} %get-tuple-element.99.q_ref, bf16[1024,128]{1,0:T(8,128)(2,1)S(1)} %pad_maximum_fusion.7.do_ref, bf16[1024,128]{1,0:T(8,128)(2,1)S(1)} %slice.501.k_ref, ...), custom_call_target="tpu_custom_call" | custom-call | flops 5368709120 | bytes 2097152 | tf_op jit(solution)/shard_map/pallas_call | solution.py:486
  277.8 2.9 fusion.80
  287.3 4.0 %collective-permute-done.69 = f32[12,1024]{1,0:T(8,128)S(1)} collective-permute-done((f32[12,1024]{1,0:T(8,128)S(1)}, f32[12,1024]{1,0:T(8,128)S(1)}, u32[]{:S(2)}, u32[]{:S(2)}) %collective-permute-start.69) | collective-permute-done | bytes 49184 | tf_op jit(solution)/shard_map/ppermute | solution.py:336
  292.2 3.4 collective-permute-done.70
  304.9 3.0 collective-permute-done.53
  309.8 4.3 %all-to-all-start.2 = ((bf16[8,32,384]{2,1,0:T(8,128)(2,1)}), bf16[8,32,384]{2,1,0:T(8,128)(2,1)S(1)}, u32[]{:S(2)}, u32[]{:S(2)}) async-start(bf16[8,32,384]{2,1,0:T(8,128)(2,1)} %bitcast.18), calls=%async_computation.2 | async-start | bytes 393216 | tf_op jit(solution)/shard_map/all_to_all | solution.py:647
  319.4 3.1 all-to-all-done.2
  327.0 2.4 collective-permute-start.58
  351.2 6.3 %collective-permute-done.76 = f32[8,128]{1,0:T(8,128)S(1)} collective-permute-done((f32[8,128]{1,0:T(8,128)S(1)}, f32[8,128]{1,0:T(8,128)S(1)}, u32[]{:S(2)}, u32[]{:S(2)}) %collective-permute-start.76) | collective-permute-done | bytes 4128 | tf_op jit(solution)/shard_map/ppermute | solution.py:336
  357.5 3.7 collective-permute-start.77
  362.1 4.2 %collective-permute-done.77 = f32[8,128]{1,0:T(8,128)S(1)} collective-permute-done((f32[8,128]{1,0:T(8,128)S(1)}, f32[8,128]{1,0:T(8,128)S(1)}, u32[]{:S(2)}, u32[]{:S(2)}) %collective-permute-start.77) | collective-permute-done | bytes 4128 | tf_op jit(solution)/shard_map/ppermute | solution.py:336
  370.8 2.7 multiply_subtract_fusion
  (425 shorter events, 163.4 us)
Async XLA Ops:
  7.2 94.1 %all-gather.2.cloned.1.call-start = ((), (), s32[]{:S(2)}) async-start(), calls=%async_computation.4 | async-start | bytes 2162688 | tf_op jit(solution)/shard_map/all_gather | solution.py:557
  7.3 15.4 %collective-permute-start = (bf16[128,1024]{1,0:T(8,128)(2,1)}, bf16[128,1024]{1,0:T(8,128)(2,1)S(1)}, u32[]{:S(2)}, u32[]{:S(2)}) collective-permute-start(bf16[128,1024]{1,0:T(8,128)(2,1)} %bitcast.146), channel_id=1, source_target_pairs={{0,2},{2,0},{1,3},{3,1},{4,6},{6,4},{5,7},{7,5},{8,10},{10,8},{9,1... | collective-permute-start | bytes 786440 | tf_op jit(solution)/shard_map/ppermute | solution.py:336
  10.3 25.2 %collective-permute-start.1 = (bf16[128,1024]{1,0:T(8,128)(2,1)}, bf16[128,1024]{1,0:T(8,128)(2,1)S(1)}, u32[]{:S(2)}, u32[]{:S(2)}) collective-permute-start(bf16[128,1024]{1,0:T(8,128)(2,1)} %bitcast.147), channel_id=1, source_target_pairs={{0,4},{4,0},{1,5},{5,1},{2,6},{6,2},{3,7},{7,3},{8,12},{12,8},{9,1... | collective-permute-start | bytes 786440 | tf_op jit(solution)/shard_map/ppermute | solution.py:336
  12.9 22.6 %collective-permute-start.2 = (bf16[128,1024]{1,0:T(8,128)(2,1)}, bf16[128,1024]{1,0:T(8,128)(2,1)S(1)}, u32[]{:S(2)}, u32[]{:S(2)}) collective-permute-start(bf16[128,1024]{1,0:T(8,128)(2,1)} %bitcast.148), channel_id=1, source_target_pairs={{0,6},{2,4},{4,2},{6,0},{1,7},{3,5},{5,3},{7,1},{8,14},{10,12},{12... | collective-permute-start | bytes 786440 | tf_op jit(solution)/shard_map/ppermute | solution.py:336
  16.8 26.0 %all-to-all-start = ((bf16[8,40,384]{2,1,0:T(8,128)(2,1)}), bf16[8,40,384]{2,1,0:T(8,128)(2,1)S(1)}, u32[]{:S(2)}, u32[]{:S(2)}) async-start(bf16[8,40,384]{2,1,0:T(8,128)(2,1)} %pad_maximum_fusion.14), calls=%async_computation | async-start | bytes 491520 | tf_op jit(solution)/shard_map/all_to_all | solution.py:541
  36.6 24.8 %collective-permute-start.3 = (bf16[512,1024]{1,0:T(8,128)(2,1)}, bf16[512,1024]{1,0:T(8,128)(2,1)S(1)}, u32[]{:S(2)}, u32[]{:S(2)}) collective-permute-start(bf16[512,1024]{1,0:T(8,128)(2,1)} %pad_maximum_fusion), channel_id=1, source_target_pairs={{0,1},{1,0},{2,3},{3,2},{4,5},{5,4},{6,7},{7,6},{8,9},{9,8},{10,11... | collective-permute-start | bytes 3145736 | tf_op jit(solution)/shard_map/ppermute | solution.py:336
  42.8 10.1 %collective-permute-start.4 = (bf16[8,40,384]{2,1,0:T(8,128)(2,1)S(1)}, bf16[8,40,384]{2,1,0:T(8,128)(2,1)S(1)}, u32[]{:S(2)}, u32[]{:S(2)}) collective-permute-start(bf16[8,40,384]{2,1,0:T(8,128)(2,1)S(1)} %all-to-all-done), channel_id=1, source_target_pairs={{0,8},{8,0},{1,9},{9,1},{2,10},{10,2},{3,11},{11,3},{4,12},{12,4},... | collective-permute-start | bytes 737288 | tf_op jit(solution)/shard_map/ppermute | solution.py:336
  44.3 7.6 %collective-permute-start.5 = (bf16[8,40,384]{2,1,0:T(8,128)(2,1)S(1)}, bf16[8,40,384]{2,1,0:T(8,128)(2,1)S(1)}, u32[]{:S(2)}, u32[]{:S(2)}) collective-permute-start(bf16[8,40,384]{2,1,0:T(8,128)(2,1)S(1)} %all-to-all-done), channel_id=1, source_target_pairs={{0,16},{16,0},{1,17},{17,1},{2,18},{18,2},{3,19},{19,3},{4,20},{20... | collective-permute-start | bytes 737288 | tf_op jit(solution)/shard_map/ppermute | solution.py:336
  74.8 15.6 %collective-permute-start.21 = (bf16[128,1024]{1,0:T(8,128)(2,1)S(1)}, bf16[128,1024]{1,0:T(8,128)(2,1)S(1)}, u32[]{:S(2)}, u32[]{:S(2)}) collective-permute-start(bf16[128,1024]{1,0:T(8,128)(2,1)S(1)} %get-tuple-element.73), channel_id=1, source_target_pairs={{0,4},{4,0},{1,5},{5,1},{2,6},{6,2},{3,7},{7,3},{8,12},{12,8},{9,1... | collective-permute-start | bytes 786440 | tf_op jit(solution)/shard_map/ppermute | solution.py:336
  77.7 8.4 %collective-permute-start.22 = (bf16[128,1024]{1,0:T(8,128)(2,1)S(1)}, bf16[128,1024]{1,0:T(8,128)(2,1)S(1)}, u32[]{:S(2)}, u32[]{:S(2)}) collective-permute-start(bf16[128,1024]{1,0:T(8,128)(2,1)S(1)} %get-tuple-element.73), channel_id=1, source_target_pairs={{0,16},{16,0},{1,17},{17,1},{2,18},{18,2},{3,19},{19,3},{4,20},{20... | collective-permute-start | bytes 786440 | tf_op jit(solution)/shard_map/ppermute | solution.py:336
  79.6 15.2 %collective-permute-start.9 = (bf16[128,256]{1,0:T(8,128)(2,1)}, bf16[128,256]{1,0:T(8,128)(2,1)}, u32[]{:S(2)}, u32[]{:S(2)}) collective-permute-start(bf16[128,256]{1,0:T(8,128)(2,1)} %get-tuple-element.145), channel_id=1, source_target_pairs={{0,2},{2,0},{1,3},{3,1},{4,6},{6,4},{5,7},{7,5},{8,10},{10,8},{9,1... | collective-permute-start | bytes 196616 | tf_op jit(solution)/shard_map/ppermute | solution.py:336
  81.3 27.9 %all-to-all-start.1 = ((bf16[8,32,512]{2,1,0:T(8,128)(2,1)}), bf16[8,32,512]{2,1,0:T(8,128)(2,1)}, u32[]{:S(2)}, u32[]{:S(2)}) async-start(bf16[8,32,512]{2,1,0:T(8,128)(2,1)} %reshape.229), calls=%async_computation.1 | async-start | bytes 524288 | tf_op jit(solution)/shard_map/all_to_all | solution.py:561
  86.8 35.4 %collective-permute-start.23 = (bf16[64,1024]{1,0:T(8,128)(2,1)}, bf16[64,1024]{1,0:T(8,128)(2,1)S(1)}, u32[]{:S(2)}, u32[]{:S(2)}) collective-permute-start(bf16[64,1024]{1,0:T(8,128)(2,1)} %slice.405), channel_id=1, source_target_pairs={{0,4},{4,0},{1,5},{5,1},{2,6},{6,2},{3,7},{7,3},{8,12},{12,8},{9,1... | collective-permute-start | bytes 393224 | tf_op jit(solution)/shard_map/ppermute | solution.py:336
  91.0 31.2 %collective-permute-start.24 = (bf16[64,1024]{1,0:T(8,128)(2,1)}, bf16[64,1024]{1,0:T(8,128)(2,1)}, u32[]{:S(2)}, u32[]{:S(2)}) collective-permute-start(bf16[64,1024]{1,0:T(8,128)(2,1)} %slice.406), channel_id=1, source_target_pairs={{0,16},{16,0},{1,17},{17,1},{2,18},{18,2},{3,19},{19,3},{4,20},{20... | collective-permute-start | bytes 393224 | tf_op jit(solution)/shard_map/ppermute | solution.py:336
  92.3 8.9 %collective-permute-start.10 = (bf16[128,256]{1,0:T(8,128)(2,1)S(1)}, bf16[128,256]{1,0:T(8,128)(2,1)S(1)}, u32[]{:S(2)}, u32[]{:S(2)}) collective-permute-start(bf16[128,256]{1,0:T(8,128)(2,1)S(1)} %copy-done.31), channel_id=1, source_target_pairs={{0,4},{4,0},{1,5},{5,1},{2,6},{6,2},{3,7},{7,3},{8,12},{12,8},{9,1... | collective-permute-start | bytes 196616 | tf_op jit(solution)/shard_map/ppermute | solution.py:336
  92.3 8.9 %collective-permute-start.11 = (bf16[128,256]{1,0:T(8,128)(2,1)S(1)}, bf16[128,256]{1,0:T(8,128)(2,1)S(1)}, u32[]{:S(2)}, u32[]{:S(2)}) collective-permute-start(bf16[128,256]{1,0:T(8,128)(2,1)S(1)} %copy-done.30), channel_id=1, source_target_pairs={{0,6},{2,4},{4,2},{6,0},{1,7},{3,5},{5,3},{7,1},{8,14},{10,12},{12... | collective-permute-start | bytes 196616 | tf_op jit(solution)/shard_map/ppermute | solution.py:336
  104.7 9.2 %collective-permute-start.12 = (bf16[128,1024]{1,0:T(8,128)(2,1)S(1)}, bf16[128,1024]{1,0:T(8,128)(2,1)S(1)}, u32[]{:S(2)}, u32[]{:S(2)}) collective-permute-start(bf16[128,1024]{1,0:T(8,128)(2,1)S(1)} %get-tuple-element.77), channel_id=1, source_target_pairs={{0,2},{2,0},{1,3},{3,1},{4,6},{6,4},{5,7},{7,5},{8,10},{10,8},{9,1... | collective-permute-start | bytes 786440 | tf_op jit(solution)/shard_map/ppermute | solution.py:336
  106.0 7.4 %collective-permute-start.13 = (bf16[128,1024]{1,0:T(8,128)(2,1)S(1)}, bf16[128,1024]{1,0:T(8,128)(2,1)S(1)}, u32[]{:S(2)}, u32[]{:S(2)}) collective-permute-start(bf16[128,1024]{1,0:T(8,128)(2,1)S(1)} %get-tuple-element.77), channel_id=1, source_target_pairs={{0,8},{8,0},{1,9},{9,1},{2,10},{10,2},{3,11},{11,3},{4,12},{12,4},... | collective-permute-start | bytes 786440 | tf_op jit(solution)/shard_map/ppermute | solution.py:336
  109.2 21.5 %collective-permute-start.17 = (bf16[8,32,512]{2,1,0:T(8,128)(2,1)}, bf16[8,32,512]{2,1,0:T(8,128)(2,1)S(1)}, u32[]{:S(2)}, u32[]{:S(2)}) collective-permute-start(bf16[8,32,512]{2,1,0:T(8,128)(2,1)} %all-to-all-done.1), channel_id=1, source_target_pairs={{0,4},{4,0},{1,5},{5,1},{2,6},{6,2},{3,7},{7,3},{8,12},{12,8},{9,1... | collective-permute-start | bytes 786440 | tf_op jit(solution)/shard_map/ppermute | solution.py:336
  113.8 7.7 %collective-permute-start.15 = (bf16[64,1024]{1,0:T(8,128)(2,1)S(1)}, bf16[64,1024]{1,0:T(8,128)(2,1)S(1)}, u32[]{:S(2)}, u32[]{:S(2)}) collective-permute-start(bf16[64,1024]{1,0:T(8,128)(2,1)S(1)} %slice.401), channel_id=1, source_target_pairs={{0,8},{8,0},{1,9},{9,1},{2,10},{10,2},{3,11},{11,3},{4,12},{12,4},... | collective-permute-start | bytes 393224 | tf_op jit(solution)/shard_map/ppermute | solution.py:336
  122.2 17.1 %collective-permute-start.16 = (bf16[512,1024]{1,0:T(8,128)(2,1)}, bf16[512,1024]{1,0:T(8,128)(2,1)S(1)}, u32[]{:S(2)}, u32[]{:S(2)}) collective-permute-start(bf16[512,1024]{1,0:T(8,128)(2,1)} %get-tuple-element.155), channel_id=1, source_target_pairs={{0,1},{1,0},{2,3},{3,2},{4,5},{5,4},{6,7},{7,6},{8,9},{9,8},{10,11... | collective-permute-start | bytes 3145736 | tf_op jit(solution)/shard_map/ppermute | solution.py:336
  126.8 10.7 %collective-permute-start.19 = (bf16[4,32,512]{2,1,0:T(8,128)(2,1)S(1)}, bf16[4,32,512]{2,1,0:T(8,128)(2,1)}, u32[]{:S(2)}, u32[]{:S(2)}) collective-permute-start(bf16[4,32,512]{2,1,0:T(8,128)(2,1)S(1)} %slice.402), channel_id=1, source_target_pairs={{0,4},{4,0},{1,5},{5,1},{2,6},{6,2},{3,7},{7,3},{8,12},{12,8},{9,1... | collective-permute-start | bytes 393224 | tf_op jit(solution)/shard_map/ppermute | solution.py:336
  175.2 7.8 %collective-permute-start.30 = (bf16[128,1024]{1,0:T(8,128)(2,1)S(1)}, bf16[128,1024]{1,0:T(8,128)(2,1)S(1)}, u32[]{:S(2)}, u32[]{:S(2)}) collective-permute-start(bf16[128,1024]{1,0:T(8,128)(2,1)S(1)} %get-tuple-element.52), channel_id=1, source_target_pairs={{0,2},{2,0},{1,3},{3,1},{4,6},{6,4},{5,7},{7,5},{8,10},{10,8},{9,1... | collective-permute-start | bytes 786440 | tf_op jit(solution)/shard_map/ppermute | solution.py:336
  206.5 16.1 %collective-permute-start.35 = (bf16[512,1024]{1,0:T(8,128)(2,1)}, bf16[512,1024]{1,0:T(8,128)(2,1)}, u32[]{:S(2)}, u32[]{:S(2)}) collective-permute-start(bf16[512,1024]{1,0:T(8,128)(2,1)} %slice.499), channel_id=1, source_target_pairs={{0,1},{1,0},{2,3},{3,2},{4,5},{5,4},{6,7},{7,6},{8,9},{9,8},{10,11... | collective-permute-start | bytes 3145736 | tf_op jit(solution)/shard_map/ppermute | solution.py:336
  207.1 12.2 %collective-permute-start.66 = (bf16[64,1024]{1,0:T(8,128)(2,1)S(1)}, bf16[64,1024]{1,0:T(8,128)(2,1)S(1)}, u32[]{:S(2)}, u32[]{:S(2)}) collective-permute-start(bf16[64,1024]{1,0:T(8,128)(2,1)S(1)} %get-tuple-element.119), channel_id=1, source_target_pairs={{0,4},{4,0},{1,5},{5,1},{2,6},{6,2},{3,7},{7,3},{8,12},{12,8},{9,1... | collective-permute-start | bytes 393224 | tf_op jit(solution)/shard_map/ppermute | solution.py:336
  210.2 12.3 %collective-permute-start.60 = (bf16[128,512]{1,0:T(8,128)(2,1)S(1)}, bf16[128,512]{1,0:T(8,128)(2,1)S(1)}, u32[]{:S(2)}, u32[]{:S(2)}) collective-permute-start(bf16[128,512]{1,0:T(8,128)(2,1)S(1)} %get-tuple-element.120), channel_id=1, source_target_pairs={{0,16},{16,0},{1,17},{17,1},{2,18},{18,2},{3,19},{19,3},{4,20},{20... | collective-permute-start | bytes 393224 | tf_op jit(solution)/shard_map/ppermute | solution.py:336
  211.8 10.7 %collective-permute-start.62 = (bf16[128,512]{1,0:T(8,128)(2,1)S(1)}, bf16[128,512]{1,0:T(8,128)(2,1)S(1)}, u32[]{:S(2)}, u32[]{:S(2)}) collective-permute-start(bf16[128,512]{1,0:T(8,128)(2,1)S(1)} %get-tuple-element.121), channel_id=1, source_target_pairs={{0,4},{4,0},{1,5},{5,1},{2,6},{6,2},{3,7},{7,3},{8,12},{12,8},{9,1... | collective-permute-start | bytes 393224 | tf_op jit(solution)/shard_map/ppermute | solution.py:336
  220.1 31.4 %collective-permute-start.65 = (bf16[128,1024]{1,0:T(8,128)(2,1)}, bf16[128,1024]{1,0:T(8,128)(2,1)}, u32[]{:S(2)}, u32[]{:S(2)}) collective-permute-start(bf16[128,1024]{1,0:T(8,128)(2,1)} %pad_maximum_fusion.12), channel_id=1, source_target_pairs={{0,4},{4,0},{1,5},{5,1},{2,6},{6,2},{3,7},{7,3},{8,12},{12,8},{9,1... | collective-permute-start | bytes 786440 | tf_op jit(solution)/shard_map/ppermute | solution.py:336
  220.8 30.7 %collective-permute-start.67 = (bf16[128,1024]{1,0:T(8,128)(2,1)}, bf16[128,1024]{1,0:T(8,128)(2,1)}, u32[]{:S(2)}, u32[]{:S(2)}) collective-permute-start(bf16[128,1024]{1,0:T(8,128)(2,1)} %pad_maximum_fusion.13), channel_id=1, source_target_pairs={{0,16},{16,0},{1,17},{17,1},{2,18},{18,2},{3,19},{19,3},{4,20},{20... | collective-permute-start | bytes 786440 | tf_op jit(solution)/shard_map/ppermute | solution.py:336
  225.2 11.4 %collective-permute-start.38 = (bf16[64,1024]{1,0:T(8,128)(2,1)S(1)}, bf16[64,1024]{1,0:T(8,128)(2,1)S(1)}, u32[]{:S(2)}, u32[]{:S(2)}) collective-permute-start(bf16[64,1024]{1,0:T(8,128)(2,1)S(1)} %get-tuple-element.106), channel_id=1, source_target_pairs={{0,2},{2,0},{1,3},{3,1},{4,6},{6,4},{5,7},{7,5},{8,10},{10,8},{9,1... | collective-permute-start | bytes 393224 | tf_op jit(solution)/shard_map/ppermute | solution.py:336
  229.2 15.4 %collective-permute-start.61 = (bf16[256,512]{1,0:T(8,128)(2,1)S(1)}, bf16[256,512]{1,0:T(8,128)(2,1)S(1)}, u32[]{:S(2)}, u32[]{:S(2)}) collective-permute-start(bf16[256,512]{1,0:T(8,128)(2,1)S(1)} %pad_maximum_fusion.10), channel_id=1, source_target_pairs={{0,4},{4,0},{1,5},{5,1},{2,6},{6,2},{3,7},{7,3},{8,12},{12,8},{9,1... | collective-permute-start | bytes 786440 | tf_op jit(solution)/shard_map/ppermute | solution.py:336
  229.5 16.9 %collective-permute-start.63 = (bf16[256,512]{1,0:T(8,128)(2,1)S(1)}, bf16[256,512]{1,0:T(8,128)(2,1)S(1)}, u32[]{:S(2)}, u32[]{:S(2)}) collective-permute-start(bf16[256,512]{1,0:T(8,128)(2,1)S(1)} %pad_maximum_fusion.11), channel_id=1, source_target_pairs={{0,16},{16,0},{1,17},{17,1},{2,18},{18,2},{3,19},{19,3},{4,20},{20... | collective-permute-start | bytes 786440 | tf_op jit(solution)/shard_map/ppermute | solution.py:336
  237.4 16.6 %collective-permute-start.37 = (bf16[128,1024]{1,0:T(8,128)(2,1)}, bf16[128,1024]{1,0:T(8,128)(2,1)}, u32[]{:S(2)}, u32[]{:S(2)}) collective-permute-start(bf16[128,1024]{1,0:T(8,128)(2,1)} %pad_maximum_fusion.4), channel_id=1, source_target_pairs={{0,2},{2,0},{1,3},{3,1},{4,6},{6,4},{5,7},{7,5},{8,10},{10,8},{9,1... | collective-permute-start | bytes 786440 | tf_op jit(solution)/shard_map/ppermute | solution.py:336
  244.6 9.4 %collective-permute-start.39 = (bf16[128,1024]{1,0:T(8,128)(2,1)}, bf16[128,1024]{1,0:T(8,128)(2,1)}, u32[]{:S(2)}, u32[]{:S(2)}) collective-permute-start(bf16[128,1024]{1,0:T(8,128)(2,1)} %pad_maximum_fusion.5), channel_id=1, source_target_pairs={{0,8},{8,0},{1,9},{9,1},{2,10},{10,2},{3,11},{11,3},{4,12},{12,4},... | collective-permute-start | bytes 786440 | tf_op jit(solution)/shard_map/ppermute | solution.py:336
  247.2 62.7 %all-to-all-start.3 = ((bf16[8,32,512]{2,1,0:T(8,128)(2,1)}), bf16[8,32,512]{2,1,0:T(8,128)(2,1)}, u32[]{:S(2)}, u32[]{:S(2)}) async-start(bf16[8,32,512]{2,1,0:T(8,128)(2,1)} %bitcast.157), calls=%async_computation.3 | async-start | bytes 524288 | tf_op jit(solution)/shard_map/all_to_all | solution.py:629
  259.3 7.5 %collective-permute-start.41 = (bf16[128,256]{1,0:T(8,128)(2,1)S(1)}, bf16[128,256]{1,0:T(8,128)(2,1)S(1)}, u32[]{:S(2)}, u32[]{:S(2)}) collective-permute-start(bf16[128,256]{1,0:T(8,128)(2,1)S(1)} %get-tuple-element.131), channel_id=1, source_target_pairs={{0,4},{4,0},{1,5},{5,1},{2,6},{6,2},{3,7},{7,3},{8,12},{12,8},{9,1... | collective-permute-start | bytes 196616 | tf_op jit(solution)/shard_map/ppermute | solution.py:336
  267.1 34.1 %collective-permute-start.52 = (bf16[16,1,32,1024]{3,2,1,0:T(8,128)(2,1)S(1)}, bf16[16,1,32,1024]{3,2,1,0:T(8,128)(2,1)}, u32[]{:S(2)}, u32[]{:S(2)}) collective-permute-start(bf16[16,1,32,1024]{3,2,1,0:T(8,128)(2,1)S(1)} %dynamic-slice_convert_fusion), channel_id=1, source_target_pairs={{0,1},{1,0},{2,3},{3,2},{4,5},{5,4},{6,7},{7,6},{8,9},{9,8},{10,11... | collective-permute-start | bytes 3145736 | tf_op jit(solution)/shard_map/ppermute | solution.py:336
  277.4 9.3 %collective-permute-start.68 = (f32[12,1024]{1,0:T(8,128)S(1)}, f32[12,1024]{1,0:T(8,128)S(1)}, u32[]{:S(2)}, u32[]{:S(2)}) collective-permute-start(f32[12,1024]{1,0:T(8,128)S(1)} %concatenate.118), channel_id=1, source_target_pairs={{0,1},{1,0},{2,3},{3,2},{4,5},{5,4},{6,7},{7,6},{8,9},{9,8},{10,11... | collective-permute-start | bytes 147464 | tf_op jit(solution)/shard_map/ppermute | solution.py:336
  286.7 43.0 %collective-permute-start.44 = (bf16[512,1024]{1,0:T(8,128)(2,1)}, bf16[512,1024]{1,0:T(8,128)(2,1)}, u32[]{:S(2)}, u32[]{:S(2)}) collective-permute-start(bf16[512,1024]{1,0:T(8,128)(2,1)} %slice.498), channel_id=1, source_target_pairs={{0,1},{1,0},{2,3},{3,2},{4,5},{5,4},{6,7},{7,6},{8,9},{9,8},{10,11... | collective-permute-start | bytes 3145736 | tf_op jit(solution)/shard_map/ppermute | solution.py:336
  291.9 11.9 %collective-permute-start.49 = (bf16[256,384]{1,0:T(8,128)(2,1)S(1)}, bf16[256,384]{1,0:T(8,128)(2,1)S(1)}, u32[]{:S(2)}, u32[]{:S(2)}) collective-permute-start(bf16[256,384]{1,0:T(8,128)(2,1)S(1)} %pad_maximum_fusion.15), channel_id=1, source_target_pairs={{0,8},{8,0},{1,9},{9,1},{2,10},{10,2},{3,11},{11,3},{4,12},{12,4},... | collective-permute-start | bytes 589832 | tf_op jit(solution)/shard_map/ppermute | solution.py:336
  300.0 18.7 %collective-permute-start.72 = (f32[12,1024]{1,0:T(8,128)S(1)}, f32[12,1024]{1,0:T(8,128)S(1)}, u32[]{:S(2)}, u32[]{:S(2)}) collective-permute-start(f32[12,1024]{1,0:T(8,128)S(1)} %add.594), channel_id=1, source_target_pairs={{0,4},{4,0},{1,5},{5,1},{2,6},{6,2},{3,7},{7,3},{8,12},{12,8},{9,1... | collective-permute-start | bytes 147464 | tf_op jit(solution)/shard_map/ppermute | solution.py:336
  309.6 13.6 %collective-permute-start.54 = (bf16[128,1024]{1,0:T(8,128)(2,1)}, bf16[128,1024]{1,0:T(8,128)(2,1)}, u32[]{:S(2)}, u32[]{:S(2)}) collective-permute-start(bf16[128,1024]{1,0:T(8,128)(2,1)} %pad_maximum_fusion.8), channel_id=1, source_target_pairs={{0,8},{8,0},{1,9},{9,1},{2,10},{10,2},{3,11},{11,3},{4,12},{12,4},... | collective-permute-start | bytes 786440 | tf_op jit(solution)/shard_map/ppermute | solution.py:336
  309.8 12.6 %all-to-all-start.2 = ((bf16[8,32,384]{2,1,0:T(8,128)(2,1)}), bf16[8,32,384]{2,1,0:T(8,128)(2,1)S(1)}, u32[]{:S(2)}, u32[]{:S(2)}) async-start(bf16[8,32,384]{2,1,0:T(8,128)(2,1)} %bitcast.18), calls=%async_computation.2 | async-start | bytes 393216 | tf_op jit(solution)/shard_map/all_to_all | solution.py:647
  314.9 9.3 %collective-permute-start.56 = (bf16[128,1024]{1,0:T(8,128)(2,1)}, bf16[128,1024]{1,0:T(8,128)(2,1)S(1)}, u32[]{:S(2)}, u32[]{:S(2)}) collective-permute-start(bf16[128,1024]{1,0:T(8,128)(2,1)} %pad_maximum_fusion.9), channel_id=1, source_target_pairs={{0,16},{16,0},{1,17},{17,1},{2,18},{18,2},{3,19},{19,3},{4,20},{20... | collective-permute-start | bytes 786440 | tf_op jit(solution)/shard_map/ppermute | solution.py:336
  339.5 21.6 %collective-permute-start.45 = (bf16[128,1024]{1,0:T(8,128)(2,1)S(1)}, bf16[128,1024]{1,0:T(8,128)(2,1)S(1)}, u32[]{:S(2)}, u32[]{:S(2)}) collective-permute-start(bf16[128,1024]{1,0:T(8,128)(2,1)S(1)} %get-tuple-element.102), channel_id=1, source_target_pairs={{0,2},{2,0},{1,3},{3,1},{4,6},{6,4},{5,7},{7,5},{8,10},{10,8},{9,1... | collective-permute-start | bytes 786440 | tf_op jit(solution)/shard_map/ppermute | solution.py:336
  339.6 21.5 %collective-permute-start.46 = (bf16[128,1024]{1,0:T(8,128)(2,1)S(1)}, bf16[128,1024]{1,0:T(8,128)(2,1)S(1)}, u32[]{:S(2)}, u32[]{:S(2)}) collective-permute-start(bf16[128,1024]{1,0:T(8,128)(2,1)S(1)} %get-tuple-element.104), channel_id=1, source_target_pairs={{0,4},{4,0},{1,5},{5,1},{2,6},{6,2},{3,7},{7,3},{8,12},{12,8},{9,1... | collective-permute-start | bytes 786440 | tf_op jit(solution)/shard_map/ppermute | solution.py:336
  341.8 19.3 %collective-permute-start.47 = (bf16[128,1024]{1,0:T(8,128)(2,1)S(1)}, bf16[128,1024]{1,0:T(8,128)(2,1)S(1)}, u32[]{:S(2)}, u32[]{:S(2)}) collective-permute-start(bf16[128,1024]{1,0:T(8,128)(2,1)S(1)} %get-tuple-element.103), channel_id=1, source_target_pairs={{0,6},{2,4},{4,2},{6,0},{1,7},{3,5},{5,3},{7,1},{8,14},{10,12},{12... | collective-permute-start | bytes 786440 | tf_op jit(solution)/shard_map/ppermute | solution.py:336
  357.5 8.9 %collective-permute-start.77 = (f32[8,128]{1,0:T(8,128)S(1)}, f32[8,128]{1,0:T(8,128)S(1)}, u32[]{:S(2)}, u32[]{:S(2)}) collective-permute-start(f32[8,128]{1,0:T(8,128)S(1)} %add.602), channel_id=1, source_target_pairs={{0,4},{4,0},{1,5},{5,1},{2,6},{6,2},{3,7},{7,3},{8,12},{12,8},{9,1... | collective-permute-start | bytes 12296 | tf_op jit(solution)/shard_map/ppermute | solution.py:336
  (87 other events, 546.9 us)
Sparse Core Ops, SparseCore 0:
  14.6 61.6 all-gather.1
